TPU v7x, 128 devices: a whole 4x4x4 slice. The times are simulated.
128 devices in a mesh: fsdp: 32 (over z, x, core), rep: 4 (over y).
Axes of the slice: x: 4, y: 4, z: 4, core: 2. Of those that a mesh axis runs over, the one named last changes fastest.
Arguments:
- gradient: float32 [4, 2048, 16384], P('rep', 'fsdp'), may hold values from -0.6 to 0.6
- block_owner_table: int32 [4, 32], replicated, may hold values from 0 to 127, as said below
- statistics: float32 [128, 4, 2, 512, 512], P(('fsdp', 'rep')), as said below
- inverse_fourth_roots: bfloat16 [128, 4, 2, 512, 512], P(('fsdp', 'rep')), as said below
Outputs:
- direction: float32 [2048, 16384], P('fsdp', 'rep')
- new_statistics: float32 [128, 4, 2, 512, 512], P(('fsdp', 'rep'))
Inputs may be any that keep to these rules, and one draw needn't show every extreme that they name: `block_owner_table`: the 32 blocks of one row block have 32 different owners. A device owns at most 4 blocks, and some device owns exactly 4. Slot s of device o holds the statistics of the block of o that is s-th in increasing row block; slots beyond o's count of blocks are never read. Each matrix is symmetric. `inverse_fourth_roots`: laid out as statistics; slots beyond a device's count of blocks are never read. Each matrix is symmetric.
All inputs are finite; a program needn't handle non-finite values.
Results may differ from a plain program's by a relative error of at most 0.0003.
Values sent between devices are 32-bit elements; how exact they have to be, the bound alone decides.
A program may use at most 192 MiB of HBM per device.

v0:
```python
import jax
import jax.numpy as jnp
from jax import lax
from jax.sharding import PartitionSpec as P

BETA = 0.9
EPS = 1e-06


def precondition(matrix, statistic, inverse_pair):
    highest = lax.Precision.HIGHEST
    left_gram = jnp.dot(matrix, matrix.T, precision=highest, preferred_element_type=jnp.float32)
    right_gram = jnp.dot(matrix.T, matrix, precision=highest, preferred_element_type=jnp.float32)
    renewed = jnp.stack(
        [
            BETA * statistic[0] + (1.0 - BETA) * left_gram,
            BETA * statistic[1] + (1.0 - BETA) * right_gram,
        ]
    )
    left_root = inverse_pair[0].astype(jnp.float32)
    right_root = inverse_pair[1].astype(jnp.float32)
    shaped = jnp.dot(
        jnp.dot(left_root, matrix, precision=highest, preferred_element_type=jnp.float32),
        right_root,
        precision=highest,
        preferred_element_type=jnp.float32,
    )
    factor = jnp.sqrt(jnp.mean(matrix * matrix)) / jnp.sqrt(jnp.mean(shaped * shaped) + EPS)
    return (renewed, shaped * factor)


def pick_columns(row_owners, targets):
    matches = row_owners[None, :] == targets[:, None]
    column_iota = jnp.arange(row_owners.shape[0], dtype=jnp.int32)
    picked = jnp.sum(jnp.where(matches, column_iota[None, :], 0), axis=1)
    return (picked, jnp.any(matches, axis=1))


def on_device(gradient, block_owner_table, statistics, inverse_fourth_roots):
    fsdp_size = lax.axis_size("fsdp")
    rep_size = lax.axis_size("rep")
    worker_count = fsdp_size * rep_size
    fsdp_index = lax.axis_index("fsdp")
    rep_index = lax.axis_index("rep")
    self_index = fsdp_index * rep_size + rep_index
    partial_value = gradient[0]
    shard_rows = partial_value.shape[0]
    col_count = partial_value.shape[1]
    block_size = statistics.shape[3]
    col_blocks = col_count // block_size
    quarter_blocks = col_blocks // rep_size
    row_blocks = block_owner_table.shape[0]
    per_block = block_size // shard_rows
    slot_count = statistics.shape[1]
    my_row_block = fsdp_index * shard_rows // block_size
    row_owners = lax.dynamic_index_in_dim(block_owner_table, my_row_block, 0, keepdims=False)
    mine = block_owner_table == self_index
    owned_rows = jnp.any(mine, axis=1)
    owned_count = owned_rows.astype(jnp.int32)
    slot_of_row = jnp.cumsum(owned_count) - owned_count
    column_iota = jnp.arange(col_blocks, dtype=jnp.int32)
    my_column = jnp.sum(jnp.where(mine, column_iota[None, :], 0), axis=1)
    slot_match = owned_rows[None, :] & (
        slot_of_row[None, :] == jnp.arange(slot_count, dtype=jnp.int32)[:, None]
    )
    row_of_slot = jnp.sum(
        jnp.where(slot_match, jnp.arange(row_blocks, dtype=jnp.int32)[None, :], 0), axis=1
    )
    slot_live = jnp.any(slot_match, axis=1)
    picked, present = pick_columns(row_owners, jnp.arange(worker_count, dtype=jnp.int32))
    pieces = partial_value.reshape(shard_rows, col_blocks, block_size)
    outgoing = jnp.where(present[None, :, None], jnp.take(pieces, picked, axis=1), 0.0)
    arrived = lax.all_to_all(outgoing, ("fsdp", "rep"), split_axis=1, concat_axis=1, tiled=True)
    row_slices = jnp.sum(arrived.reshape(shard_rows, fsdp_size, rep_size, block_size), axis=2)
    assembled = (
        row_slices.reshape(shard_rows, row_blocks, per_block, block_size)
        .transpose(1, 2, 0, 3)
        .reshape(row_blocks, block_size, block_size)
    )
    slot_blocks = jnp.take(assembled, row_of_slot, axis=0)

    def one_slot(record):
        matrix, statistic, inverse_pair, live = record
        return lax.cond(
            live,
            lambda: precondition(matrix, statistic, inverse_pair),
            lambda: (jnp.zeros(statistic.shape, jnp.float32), jnp.zeros(matrix.shape, jnp.float32)),
        )

    renewed, updated = lax.map(
        one_slot, (slot_blocks, statistics[0], inverse_fourth_roots[0], slot_live)
    )
    new_statistics = renewed[None]
    row_updates = jnp.where(owned_rows[:, None, None], jnp.take(updated, slot_of_row, axis=0), 0.0)
    by_shard = row_updates.reshape(row_blocks, per_block, shard_rows, block_size).reshape(
        fsdp_size, shard_rows, block_size
    )
    row_block_of_shard = jnp.arange(fsdp_size, dtype=jnp.int32) * shard_rows // block_size
    shard_owned = owned_rows[row_block_of_shard]
    shard_quarter = my_column[row_block_of_shard] // quarter_blocks
    send_mask = shard_owned[:, None] & (
        shard_quarter[:, None] == jnp.arange(rep_size, dtype=jnp.int32)[None, :]
    )
    returning = jnp.where(send_mask[:, :, None, None], by_shard[:, None, :, :], 0.0).reshape(
        worker_count, shard_rows, block_size
    )
    came_back = lax.all_to_all(returning, ("fsdp", "rep"), split_axis=0, concat_axis=0, tiled=True)
    quarter_owners = lax.dynamic_slice_in_dim(
        row_owners, rep_index * quarter_blocks, quarter_blocks
    )
    final_pieces = jnp.take(came_back, quarter_owners, axis=0)
    direction = final_pieces.transpose(1, 0, 2).reshape(shard_rows, quarter_blocks * block_size)
    return (direction, new_statistics)


def solution(mesh):
    in_specs = (
        P("rep", "fsdp", None),
        P(),
        P(("fsdp", "rep"), None, None, None, None),
        P(("fsdp", "rep"), None, None, None, None),
    )
    out_specs = (P("fsdp", "rep"), P(("fsdp", "rep"), None, None, None, None))
    return jax.shard_map(
        on_device, mesh=mesh, in_specs=in_specs, out_specs=out_specs, check_vma=False
    )
```

profile of v0, /device:TPU:0, one launch (start us, length us, event | category | flops | bytes accessed | tf_op | source)
XLA Modules:
  0.0 582.7 jit_solution(4982627217610210504)
XLA Ops:
  0.7 0.7 dynamic-slice_bitcast_fusion.4
  1.5 4.6 copy.12
  6.1 4.4 copy.9
  10.6 11.7 %gather_fusion = f32[128,64,512]{2,1,0:T(8,128)} fusion(f32[64,32,512]{2,0,1:T(8,128)} %copy.9, s32[1024]{0:T(1024)S(1)} %pad_clamp_fusion.3), kind=kCustom, calls=%fused_computation.2 | custom fusion | bytes 33554944 | tf_op jit(solution)/shard_map/jit(_take)/gather | solution.py:72
  22.3 12.5 %select_bitcast_fusion = f32[64,128,512]{2,0,1:T(8,128)} fusion(f32[128,64,512]{2,1,0:T(8,128)} %gather_fusion, pred[128]{0:T(512)(128)(4,1)S(1)} %fusion.19, pred[128]{0:T(512)(128)(4,1)S(1)} %compare_and_fusion.2), kind=kLoop, calls=%fused_computation.37 | loop fusion | flops 8388608 | bytes 33554688 | tf_op jit(solution)/shard_map/jit(_where)/select_n | solution.py:72
  34.7 11.8 %all-to-all-start = ((f32[64,128,512]{2,0,1:T(8,128)}), f32[64,128,512]{2,0,1:T(8,128)}, u32[]{:S(2)}, u32[]{:S(2)}) async-start(f32[64,128,512]{2,0,1:T(8,128)} %select_bitcast_fusion), calls=%async_computation | async-start | bytes 33554432 | tf_op jit(solution)/shard_map/all_to_all | solution.py:73
  46.7 0.1 reduce_or.27
  46.8 0.2 reduce-window.7
  47.0 0.6 fusion.26
  47.6 2.4 select_bitcast_fusion.2
  50.1 0.6 fusion.27
  50.7 2.4 and_select_fusion
  53.6 198.1 %all-to-all-done = f32[64,128,512]{2,0,1:T(8,128)} async-done(((f32[64,128,512]{2,0,1:T(8,128)}), f32[64,128,512]{2,0,1:T(8,128)}, u32[]{:S(2)}, u32[]{:S(2)}) %all-to-all-start) | async-done | bytes 16777248 | tf_op jit(solution)/shard_map/all_to_all | solution.py:73
  251.7 10.4 %bitcast_reduce_fusion = f32[64,32,512]{2,0,1:T(8,128)} fusion(f32[64,128,512]{2,0,1:T(8,128)} %all-to-all-done), kind=kLoop, calls=%fused_computation.36 | loop fusion | flops 3145728 | bytes 20971520 | tf_op jit(solution)/shard_map/reduce_sum | solution.py:74
  262.0 5.0 gather_fusion.2
  267.0 4.8 broadcast_select_fusion
  271.8 16.4 %while.13 = (s32[]{:T(128)}, f32[4,2,512,512]{3,2,1,0:T(8,128)}, f32[4,512,512]{2,1,0:T(8,128)}, pred[4]{0:T(512)(128)(4,1)S(1)}, f32[4,2,512,512]{3,2,1,0:T(8,1...) while((s32[]{:T(128)}, f32[4,2,512,512]{3,2,1,0:T(8,128)}, ...), condition=%wide.region_13.15_spmd.clone, body=%wide.region_8.14_spmd.sunk.clone | while | flops 6445858816 | bytes 25170668 | solution.py:90
  271.8 0.6 dynamic_slice.64
  272.9 0.4 conditional.3
  272.9 0.2 broadcast_in_dim.131
  273.2 0.1 broadcast_in_dim.132
  273.3 1.5 constant_dynamic-update-slice_fusion.6
  274.8 1.1 constant_dynamic-update-slice_fusion.7
  275.9 0.6 dynamic_slice.64
  277.0 0.4 conditional.3
  277.0 0.2 broadcast_in_dim.131
  277.3 0.1 broadcast_in_dim.132
  277.4 1.5 constant_dynamic-update-slice_fusion.6
  278.9 1.1 constant_dynamic-update-slice_fusion.7
  280.0 0.6 dynamic_slice.64
  281.1 0.4 conditional.3
  281.1 0.2 broadcast_in_dim.131
  281.4 0.1 broadcast_in_dim.132
  281.5 1.5 constant_dynamic-update-slice_fusion.6
  283.0 1.0 constant_dynamic-update-slice_fusion.7
  284.1 0.6 dynamic_slice.64
  285.2 0.4 conditional.3
  285.2 0.2 broadcast_in_dim.131
  285.6 1.5 constant_dynamic-update-slice_fusion.6
  287.1 1.1 constant_dynamic-update-slice_fusion.7
  288.2 4.9 gather_fusion.3
  293.1 2.8 select_select_fusion
  295.9 8.1 %bitcast_select_fusion = f32[128,64,512]{2,1,0:T(8,128)} fusion(f32[32,64,512]{2,1,0:T(8,128)S(1)} %bitcast.94, pred[128]{0:T(512)(128)(4,1)S(1)} %and.87), kind=kLoop, calls=%fused_computation.35 | loop fusion | flops 4194304 | bytes 20971648 | tf_op jit(solution)/shard_map/jit(_where)/select_n | solution.py:104
  304.0 67.2 %all-to-all-start.1 = ((f32[128,64,512]{2,1,0:T(8,128)}), f32[128,64,512]{2,1,0:T(8,128)}, u32[]{:S(2)}, u32[]{:S(2)}) async-start(f32[128,64,512]{2,1,0:T(8,128)} %bitcast_select_fusion), calls=%async_computation.1 | async-start | bytes 33554432 | tf_op jit(solution)/shard_map/all_to_all | solution.py:107
  371.3 203.7 %all-to-all-done.1 = f32[128,64,512]{2,1,0:T(8,128)} async-done(((f32[128,64,512]{2,1,0:T(8,128)}), f32[128,64,512]{2,1,0:T(8,128)}, u32[]{:S(2)}, u32[]{:S(2)}) %all-to-all-start.1) | async-done | bytes 16777248 | tf_op jit(solution)/shard_map/all_to_all | solution.py:107
  575.0 6.4 %gather_fusion.1 = f32[8,64,512]{2,1,0:T(8,128)S(1)} fusion(f32[128,64,512]{2,1,0:T(8,128)} %all-to-all-done.1, s32[1024]{0:T(1024)S(1)} %pad_clamp_fusion), kind=kCustom, calls=%fused_computation.3 | custom fusion | bytes 2097184 | tf_op jit(solution)/shard_map/jit(_take)/gather | solution.py:111
  581.4 0.2 select_bitcast_fusion.1
  581.6 1.1 copy.11
  (25 shorter events, 1.1 us)
Async XLA Ops:
  34.7 11.9 %copy-start = (s32[4,32]{1,0:T(4,128)S(1)}, s32[4,32]{1,0:T(4,128)}, u32[]{:S(2)}) copy-start(s32[4,32]{1,0:T(4,128)} %param.11) | copy-start | bytes 1540
  34.7 216.9 %all-to-all-start = ((f32[64,128,512]{2,0,1:T(8,128)}), f32[64,128,512]{2,0,1:T(8,128)}, u32[]{:S(2)}, u32[]{:S(2)}) async-start(f32[64,128,512]{2,0,1:T(8,128)} %select_bitcast_fusion), calls=%async_computation | async-start | bytes 33554432 | tf_op jit(solution)/shard_map/all_to_all | solution.py:73
  304.0 271.0 %all-to-all-start.1 = ((f32[128,64,512]{2,1,0:T(8,128)}), f32[128,64,512]{2,1,0:T(8,128)}, u32[]{:S(2)}, u32[]{:S(2)}) async-start(f32[128,64,512]{2,1,0:T(8,128)} %bitcast_select_fusion), calls=%async_computation.1 | async-start | bytes 33554432 | tf_op jit(solution)/shard_map/all_to_all | solution.py:107
where the time goes:
time: 594 us; the launch traced here: 583 us
  waiting for transfers between devices  402 us (68%)
  starting transfers between devices  79 us (13%)
  local copies, waits for them, and re-layouts  54.1 us (9%)
  other arithmetic  44.6 us (8%)
    all_to_all x1, waiting for transfers between devices, on_device(): lax.all_to_all(returning, ('fsdp', 'rep'), split_axis=0, concat_axis=0, t...  204 us
    all_to_all x1, waiting for transfers between devices, on_device(): lax.all_to_all(outgoing, ('fsdp', 'rep'), split_axis=1, concat_axis=1, ti...  198 us
    all_to_all x1, starting transfers between devices, on_device(): lax.all_to_all(returning, ('fsdp', 'rep'), split_axis=0, concat_axis=0, t...  67.2 us
    select_n x1, other arithmetic, on_device(): jnp.where(present[None, :, None], jnp.take(pieces, picked, axis=1), 0.0)  12.5 us
  transfers between devices with their start and end apart: 2, of which 2 were waited for; matrix products, arithmetic and copies ran while one was open for 1% of the time, Pallas kernels for 0%

commit v1 on v0

v1 whole, which is shorter than its diff:
```python
import functools

import jax
import jax.numpy as jnp
from jax import lax
from jax.experimental import pallas as pl
from jax.experimental.pallas import tpu as pltpu
from jax.sharding import PartitionSpec as P

BETA = 0.9
EPS = 1e-06


def split(value):
    high = value.astype(jnp.bfloat16)
    low = (value - high.astype(jnp.float32)).astype(jnp.bfloat16)
    return high, low


def dot(a, b):
    return jnp.dot(a, b, preferred_element_type=jnp.float32)


def dot_t(a, b):
    return lax.dot_general(a, b, (((1,), (1,)), ((), ())), preferred_element_type=jnp.float32)


def block_kernel(row_ref, live_ref, g_ref, stat_ref, root_ref, new_ref, out_ref):
    live = live_ref[pl.program_id(0)] > 0

    @pl.when(live)
    def _():
        matrix = g_ref[0]
        size = matrix.shape[0]
        high, low = split(matrix)
        half = high * jnp.bfloat16(0.5)
        left = dot_t(high, half) + dot_t(high, low)
        new_ref[0, 0, 0] = BETA * stat_ref[0, 0, 0] + (1.0 - BETA) * (left + left.T)
        high_t = high.T
        right = dot(high_t, half) + dot(high_t, low)
        new_ref[0, 0, 1] = BETA * stat_ref[0, 0, 1] + (1.0 - BETA) * (right + right.T)
        left_root = root_ref[0, 0, 0]
        right_root = root_ref[0, 0, 1]
        t_high, t_low = split(dot(left_root, high) + dot(left_root, low))
        shaped = dot(t_high, right_root) + dot(t_low, right_root)
        count = size * size
        square_g = jnp.sum(matrix * matrix, keepdims=True) / count
        square_s = jnp.sum(shaped * shaped, keepdims=True) / count
        out_ref[0] = shaped * (jnp.sqrt(square_g) / jnp.sqrt(square_s + EPS))

    @pl.when(jnp.logical_not(live))
    def _():
        new_ref[...] = jnp.zeros_like(new_ref)
        out_ref[...] = jnp.zeros_like(out_ref)


def precondition(row_of_slot, live, blocks, statistics, roots):
    slots, size = statistics.shape[1], statistics.shape[3]
    square = (1, size, size)
    pair = (1, 1, 2, size, size)
    by_row = pl.BlockSpec(square, lambda s, row, live: (row[s], 0, 0))
    by_slot = pl.BlockSpec(pair, lambda s, row, live: (0, s, 0, 0, 0))
    return pl.pallas_call(
        block_kernel,
        grid_spec=pltpu.PrefetchScalarGridSpec(
            num_scalar_prefetch=2,
            grid=(slots,),
            in_specs=[by_row, by_slot, by_slot],
            out_specs=[by_slot, by_row],
        ),
        out_shape=(
            jax.ShapeDtypeStruct(statistics.shape, jnp.float32),
            jax.ShapeDtypeStruct(blocks.shape, jnp.float32),
        ),
        compiler_params=pltpu.CompilerParams(vmem_limit_bytes=48 * 2**20),
        name="precondition",
    )(row_of_slot, live, blocks, statistics, roots)


def slot_order(mine):
    owned = jnp.any(mine, axis=1)
    count = owned.astype(jnp.int32)
    free = 1 - count
    slot_of_row = jnp.where(
        owned, jnp.cumsum(count) - count, jnp.sum(count) + jnp.cumsum(free) - free
    )
    rows = jnp.arange(count.shape[0], dtype=jnp.int32)
    match = slot_of_row[None, :] == rows[:, None]
    row_of_slot = jnp.sum(jnp.where(match, rows[None, :], 0), axis=1)
    live = (rows < jnp.sum(count)).astype(jnp.int32)
    return row_of_slot, live


def on_device(gradient, block_owner_table, statistics, inverse_fourth_roots):
    fsdp_size = lax.axis_size("fsdp")
    rep_size = lax.axis_size("rep")
    workers = fsdp_size * rep_size
    fsdp_index = lax.axis_index("fsdp")
    rep_index = lax.axis_index("rep")
    size = statistics.shape[3]
    row_blocks, col_blocks = block_owner_table.shape
    shard_rows = gradient.shape[1]
    piece_rows = shard_rows // rep_size
    table = block_owner_table

    row_owners = lax.dynamic_index_in_dim(
        table, fsdp_index * shard_rows // size, 0, keepdims=False
    )
    row_of_slot, live = slot_order(table == fsdp_index * rep_size + rep_index)
    matches = row_owners[None, :] == jnp.arange(workers, dtype=jnp.int32)[:, None]
    columns = jnp.arange(col_blocks, dtype=jnp.int32)
    picked = jnp.sum(jnp.where(matches, columns[None, :], 0), axis=1)

    summed = lax.psum_scatter(gradient[0], "rep", scatter_dimension=0, tiled=True)
    pieces = summed.reshape(piece_rows, col_blocks, size).transpose(1, 0, 2)
    outgoing = jnp.take(pieces, picked, axis=0)
    arrived = lax.all_to_all(outgoing, ("fsdp", "rep"), split_axis=0, concat_axis=0, tiled=True)
    blocks = arrived.reshape(row_blocks, size, size)
    new_statistics, updated = precondition(
        row_of_slot, live, blocks, statistics, inverse_fourth_roots
    )
    returning = updated.reshape(workers, piece_rows, size)
    came_back = lax.all_to_all(returning, ("fsdp", "rep"), split_axis=0, concat_axis=0, tiled=True)
    ordered = jnp.take(came_back, row_owners, axis=0)
    quarter = lax.all_to_all(ordered, "rep", split_axis=0, concat_axis=1, tiled=True)
    direction = quarter.transpose(1, 0, 2).reshape(shard_rows, -1)
    return (direction, new_statistics)


def solution(mesh):
    in_specs = (
        P("rep", "fsdp", None),
        P(),
        P(("fsdp", "rep"), None, None, None, None),
        P(("fsdp", "rep"), None, None, None, None),
    )
    out_specs = (P("fsdp", "rep"), P(("fsdp", "rep"), None, None, None, None))
    return jax.shard_map(
        on_device, mesh=mesh, in_specs=in_specs, out_specs=out_specs, check_vma=False
    )
```

time: 594 us -> 233 us (0.39); the launches traced: 583 us -> 232 us
  waiting for transfers between devices: 402 us -> 153 us
  starting transfers between devices: 79 us -> 16.1 us
  local copies, waits for them, and re-layouts: 54.1 us -> 11.1 us
  other arithmetic: 44.6 us -> 7.37 us
  blocking collectives: 0 us -> 18.7 us
  between operations: 0.79 us -> 14.2 us
  Pallas kernels: 0 us -> 12.1 us
    all_to_all x1, waiting for transfers between devices: 204 us -> 51.5 us  [on_device(): lax.all_to_all(returning, ('fsdp', 'rep'), split_axis=0, concat_axis=0, t...]
    all_to_all x1, waiting for transfers between devices: 198 us -> 48.9 us  [on_device(): lax.all_to_all(outgoing, ('fsdp', 'rep'), split_axis=0, concat_axis=0, ti...]
    all_to_all x1, starting transfers between devices: 67.2 us -> 7.13 us  [on_device(): lax.all_to_all(returning, ('fsdp', 'rep'), split_axis=0, concat_axis=0, t...]
    reduce_scatter x0 -> x1, waiting for transfers between devices: none -> 51.7 us  [on_device(): lax.psum_scatter(gradient[0], 'rep', scatter_dimension=0, tiled=True)]
    select_n x9 -> x5, other arithmetic: 30.6 us -> 5.36 us  [the longest x2 4.56 us: on_device(): outgoing = jnp.take(pieces, picked, axis=0)]
    gather x6 -> x2, local copies, waits for them, and re-layouts: 29.2 us -> 5.63 us  [the longest x1 2.83 us: on_device(): outgoing = jnp.take(pieces, picked, axis=0)]
    all_to_all x0 -> x1, blocking collectives: none -> 18.7 us  [on_device(): lax.all_to_all(ordered, 'rep', split_axis=0, concat_axis=1, tiled=True)]
    pallas_call x0 -> x1, Pallas kernels: none -> 12.1 us  [precondition(): pl.pallas_call(block_kernel, grid_spec=pltpu.PrefetchScalarGridSpec(num_s...]
  transfers between devices with their start and end apart: 2 -> 3, of which waited for: 2 -> 3; matrix products, arithmetic and copies ran while one was open for 1% -> 1% of each run, Pallas kernels for 0% -> 0%
where the time goes in v1:
time: 233 us; the launch traced here: 232 us
  waiting for transfers between devices  153 us (66%)
  blocking collectives  18.7 us (8%)
  starting transfers between devices  16.1 us (7%)
  between operations  14.2 us (6%)
  Pallas kernels  12.1 us (5%)
  local copies, waits for them, and re-layouts  11.1 us (5%)
  other arithmetic  7.37 us (3%)
    reduce_scatter x1, waiting for transfers between devices, on_device(): lax.psum_scatter(gradient[0], 'rep', scatter_dimension=0, tiled=True)  51.7 us
    all_to_all x1, waiting for transfers between devices, on_device(): lax.all_to_all(returning, ('fsdp', 'rep'), split_axis=0, concat_axis=0, t...  51.5 us
    all_to_all x1, waiting for transfers between devices, on_device(): lax.all_to_all(outgoing, ('fsdp', 'rep'), split_axis=0, concat_axis=0, ti...  48.9 us
    all_to_all x1, blocking collectives, on_device(): lax.all_to_all(ordered, 'rep', split_axis=0, concat_axis=1, tiled=True)  18.7 us
    pallas_call x1, Pallas kernels, precondition(): pl.pallas_call(block_kernel, grid_spec=pltpu.PrefetchScalarGridSpec(num_s...  12.1 us
    all_to_all x1, starting transfers between devices, on_device(): lax.all_to_all(outgoing, ('fsdp', 'rep'), split_axis=0, concat_axis=0, ti...  8.91 us
    all_to_all x1, starting transfers between devices, on_device(): lax.all_to_all(returning, ('fsdp', 'rep'), split_axis=0, concat_axis=0, t...  7.13 us
  transfers between devices with their start and end apart: 3, of which 3 were waited for; matrix products, arithmetic and copies ran while one was open for 1% of the time, Pallas kernels for 0%

profile of v1, /device:TPU:0, one launch (start us, length us, event | category | flops | bytes accessed | tf_op | source)
XLA Modules:
  0.0 232.2 jit_solution(3003168871674203817)
XLA Ops:
  7.2 0.0 copy-start.1
  7.2 0.0 reduce-scatter.2.cloned.1.call-start
  7.2 0.7 reduce-scatter.2.cloned.1.call-update
  7.9 0.0 copy-done.1
  8.0 0.1 select_reduce_fusion
  8.1 51.7 %reduce-scatter.2.cloned.1.call-done = f32[16,16384]{1,0:T(8,128)} async-done(((f32[64,16384]{1,0:T(8,128)}), f32[16,16384]{1,0:T(8,128)}) %reduce-scatter.2.cloned.1.call-update) | async-done | bytes 1048592 | tf_op jit(solution)/shard_map/reduce_scatter | solution.py:114
  59.7 1.3 copy.15
  61.1 2.8 %gather_fusion = f32[128,16,512]{2,1,0:T(8,128)} fusion(f32[32,16,512]{2,1,0:T(8,128)S(1)} %bitcast.42, s32[1024]{0:T(1024)S(1)} %pad_clamp_fusion.1), kind=kCustom, calls=%fused_computation | custom fusion | bytes 8389120 | tf_op jit(solution)/shard_map/jit(_take)/gather | solution.py:116
  63.9 4.6 %broadcast_select_fusion = f32[128,16,512]{2,1,0:T(8,128)} fusion(f32[128,16,512]{2,1,0:T(8,128)} %gather_fusion, pred[128]{0:T(512)(128)(4,1)S(1)} %compare_and_fusion), kind=kLoop, calls=%fused_computation.2 | loop fusion | flops 1048576 | bytes 8388736 | tf_op jit(solution)/shard_map/jit(_take)/select_n | solution.py:116
  68.4 8.9 %all-to-all-start = ((f32[128,16,512]{2,1,0:T(8,128)}), f32[128,16,512]{2,1,0:T(8,128)}, u32[]{:S(2)}, u32[]{:S(2)}) async-start(f32[128,16,512]{2,1,0:T(8,128)} %broadcast_select_fusion), calls=%async_computation.1 | async-start | bytes 8388608 | tf_op jit(solution)/shard_map/all_to_all | solution.py:117
  77.4 0.1 compare_reduce_fusion
  77.5 0.2 reduce-window.16
  77.7 0.2 reduce-window.17
  77.9 0.6 convert_reduce_fusion
  78.5 0.6 compare_convert_fusion.live_ref
  79.2 0.7 fusion.2
  79.8 0.1 select_reduce_fusion.1.row_ref
  79.9 48.9 %all-to-all-done = f32[128,16,512]{2,1,0:T(8,128)} async-done(((f32[128,16,512]{2,1,0:T(8,128)}), f32[128,16,512]{2,1,0:T(8,128)}, u32[]{:S(2)}, u32[]{:S(2)}) %all-to-all-start) | async-done | bytes 4194336 | tf_op jit(solution)/shard_map/all_to_all | solution.py:117
  128.9 12.1 %precondition.1 = (f32[1,4,2,512,512]{4,3,2,1,0:T(8,128)}, f32[4,512,512]{2,1,0:T(8,128)S(1)}) custom-call(s32[4]{0:T(128)S(1)} %select_reduce_fusion.1.row_ref, s32[4]{0:T(128)S(1)} %compare_convert_fusion.live_ref, f32[4,512,512]{2,1,0:T(8,128)} %bitcast.8.g_ref, f32[1,4,2,512,512]{4,3,2,1,0:T(8,128)} %stat_ref.1, bf16[1,4,2,512,512]{4,3,2,1,0:T(8,128)(2,1)} %root_ref.1), custom_call_target="tpu_custom_call" | custom-call | tf_op jit(solution)/shard_map/precondition/pallas_call | solution.py:63
  140.9 0.0 copy-start
  141.0 2.0 copy-done
  142.9 7.1 %all-to-all-start.1 = ((f32[128,16,512]{2,1,0:T(8,128)}), f32[128,16,512]{2,1,0:T(8,128)}, u32[]{:S(2)}, u32[]{:S(2)}) async-start(f32[128,16,512]{2,1,0:T(8,128)} %bitcast.41), calls=%async_computation.2 | async-start | bytes 8388608 | tf_op jit(solution)/shard_map/all_to_all | solution.py:123
  150.1 51.5 %all-to-all-done.1 = f32[128,16,512]{2,1,0:T(8,128)} async-done(((f32[128,16,512]{2,1,0:T(8,128)}), f32[128,16,512]{2,1,0:T(8,128)}, u32[]{:S(2)}, u32[]{:S(2)}) %all-to-all-start.1) | async-done | bytes 4194336 | tf_op jit(solution)/shard_map/all_to_all | solution.py:123
  201.6 2.8 %gather_fusion.1 = f32[32,16,512]{2,1,0:T(8,128)S(1)} fusion(f32[128,16,512]{2,1,0:T(8,128)} %all-to-all-done.1, s32[1024]{0:T(1024)S(1)} %pad_clamp_fusion), kind=kCustom, calls=%fused_computation.1 | custom fusion | bytes 2097280 | tf_op jit(solution)/shard_map/jit(_take)/gather | solution.py:124
  204.4 0.1 broadcast_select_fusion.1
  204.5 18.7 %all_to_all.28 = f32[32,16,512]{2,1,0:T(8,128)S(1)} all-to-all(f32[32,16,512]{2,1,0:T(8,128)S(1)} %broadcast_select_fusion.1), channel_id=1, replica_groups=mesh['fsdp'=32,'rep'=4] {'rep'}, dimensions={0} | all-to-all | bytes 2097152 | tf_op jit(solution)/shard_map/all_to_all | solution.py:125
  223.2 0.6 copy.11
  223.8 1.6 copy.13
  (8 shorter events, 0.1 us)
Async XLA Ops:
  7.2 0.8 copy-start.1
  7.2 52.6 %reduce-scatter.2.cloned.1.call-start = ((), (), s32[]{:S(2)}) async-start(), calls=%async_computation.4 | async-start | bytes 5242880 | tf_op jit(solution)/shard_map/reduce_scatter | solution.py:114
  68.4 60.4 %all-to-all-start = ((f32[128,16,512]{2,1,0:T(8,128)}), f32[128,16,512]{2,1,0:T(8,128)}, u32[]{:S(2)}, u32[]{:S(2)}) async-start(f32[128,16,512]{2,1,0:T(8,128)} %broadcast_select_fusion), calls=%async_computation.1 | async-start | bytes 8388608 | tf_op jit(solution)/shard_map/all_to_all | solution.py:117
  140.9 2.0 copy-start
  142.9 58.6 %all-to-all-start.1 = ((f32[128,16,512]{2,1,0:T(8,128)}), f32[128,16,512]{2,1,0:T(8,128)}, u32[]{:S(2)}, u32[]{:S(2)}) async-start(f32[128,16,512]{2,1,0:T(8,128)} %bitcast.41), calls=%async_computation.2 | async-start | bytes 8388608 | tf_op jit(solution)/shard_map/all_to_all | solution.py:123
Sparse Core Ops, SparseCore 0:
  10.4 49.2 reduce-scatter.1

commit v2 on v1

--- a/solution.py
+++ b/solution.py
@@ -1,4 +1,5 @@
 import functools
+import itertools
 
 import jax
 import jax.numpy as jnp
@@ -9,6 +10,252 @@
 
 BETA = 0.9
 EPS = 1e-06
+MESH = pl.DeviceIdType.MESH
+RING = 4
+CORES = 2
+PARTS = 4
+
+
+def far_first():
+    seen, orbits = set(), []
+    for start in itertools.product(range(RING), repeat=3):
+        if start in seen:
+            continue
+        orbit, turned = [], start
+        for _ in range(3):
+            for offset in (turned, tuple(-v % RING for v in turned)):
+                if offset not in orbit:
+                    orbit.append(offset)
+            turned = turned[1:] + turned[:1]
+        seen.update(orbit)
+        orbits.append(orbit)
+    orbits.sort(key=lambda orbit: -sum(min(v, RING - v) for v in orbit[0]))
+    order = [(z, x, c, y) for orbit in orbits for c in range(CORES) for z, x, y in orbit]
+    return [offset for offset in order if any(offset)]
+
+
+ORDER = far_first()
+
+
+class Place:
+    def __init__(self):
+        fsdp, self.y = lax.axis_index("fsdp"), lax.axis_index("rep")
+        self.z, self.x, self.c = fsdp // 8, fsdp // 2 % 4, fsdp % 2
+        self.shard = fsdp % 8
+        self.index = fsdp * RING + self.y
+        self.zs = [lax.rem(self.z + d, RING) for d in range(RING)]
+        self.xs = [lax.rem(self.x + d, RING) * CORES for d in range(RING)]
+        self.cs = [self.c, 1 - self.c]
+        self.ys = [lax.rem(self.y + d, RING) for d in range(RING)]
+
+    def at(self, dz, dx, dc, dy):
+        shard = self.xs[dx] + self.cs[dc]
+        z, y = self.zs[dz], self.ys[dy]
+        return z, shard * RING + y, (z * 8 + shard, y)
+
+    def line(self, dy):
+        return {"rep": self.ys[dy]}
+
+
+def greet_all(place):
+    barrier = pltpu.get_barrier_semaphore()
+    for offset in ORDER:
+        pl.semaphore_signal(barrier, inc=1, device_id=place.at(*offset)[2], device_id_type=MESH)
+    pl.semaphore_wait(barrier, len(ORDER))
+
+
+def send(src, dst, sent, landed, device):
+    copy = pltpu.make_async_remote_copy(
+        src_ref=src,
+        dst_ref=dst,
+        send_sem=sent,
+        recv_sem=landed,
+        device_id=device,
+        device_id_type=MESH,
+    )
+    copy.start()
+
+
+def await_bytes(like, semaphore):
+    pltpu.make_async_copy(like, like, semaphore).wait()
+
+
+def dispatch_kernel(
+    picked_ref, grad_ref, out_ref,
+    near, mine, relay, coming, pieces, stage,
+    load_sem, sent_sem, relay_sent_sem, relay_sem, coming_sem, out_sent_sem, out_sem,
+):
+    place = Place()
+    rows, half = mine.shape[0], mine.shape[1] // 2
+    width = half // PARTS
+    size = stage.shape[2]
+
+    def quarter(dy):
+        return pl.ds(pl.multiple_of(place.ys[dy] * rows, rows), rows)
+
+    def grad(dy, side, part=None):
+        start, count = (side * half, half) if part is None else (side * half + part * width, width)
+        return grad_ref.at[0, quarter(dy), pl.ds(start, count)]
+
+    loads = [
+        pltpu.make_async_copy(grad(1, 0), near.at[0], load_sem.at[0]),
+        pltpu.make_async_copy(grad(3, 1), near.at[1], load_sem.at[1]),
+        pltpu.make_async_copy(grad_ref.at[0, quarter(0)], mine, load_sem.at[2]),
+    ]
+    for load in loads:
+        load.start()
+    greet_all(place)
+
+    ways = ((1, 0), (3, 1))
+    for part in range(PARTS):
+        for to, side in ways:
+            send(
+                grad(2, side, part), relay.at[side, :, pl.ds(part * width, width)],
+                sent_sem, relay_sem.at[side, part], place.line(to),
+            )
+    for part in range(PARTS):
+        for to, side in ways:
+            columns = pl.ds((1 - side) * half + part * width, width)
+            send(
+                grad(to, 1 - side, part), coming.at[side, :, columns],
+                sent_sem, coming_sem.at[side, 1 - side, part], place.line(to),
+            )
+    for load in loads:
+        load.wait()
+    for part in range(PARTS):
+        for to, side in ways:
+            here = pl.ds(part * width, width)
+            block = relay.at[side, :, here]
+            await_bytes(block, relay_sem.at[side, part])
+            relay[side, :, here] += near[side, :, here]
+            columns = pl.ds(side * half + part * width, width)
+            send(
+                block, coming.at[side, :, columns],
+                relay_sent_sem, coming_sem.at[side, side, part], place.line(to),
+            )
+    for side in range(2):
+        for part in range(PARTS):
+            columns = pl.ds((1 - side) * half + part * width, width)
+            await_bytes(coming.at[side, :, columns], coming_sem.at[side, 1 - side, part])
+            mine[:, columns] += coming[side, :, columns]
+    for part in range(PARTS):
+        for side in range(2):
+            start = side * half + part * width
+            columns = pl.ds(start, width)
+            await_bytes(coming.at[side, :, columns], coming_sem.at[side, side, part])
+            for column in range(start, start + width, size):
+                at = pl.ds(column, size)
+                pieces[column // size] = mine[:, at] + coming[side, :, at]
+
+    chunk = pl.ds(pl.multiple_of((place.shard * RING + place.y) * rows, rows), rows)
+    landing = out_ref.at[place.z, chunk]
+    for offset in ORDER:
+        z, k, device = place.at(*offset)
+        target = z * 32 + k
+        stage[target] = pieces[picked_ref[target]]
+        send(stage.at[target], landing, out_sent_sem, out_sem.at[place.z], device)
+    stage[place.index] = pieces[picked_ref[place.index]]
+    pltpu.make_async_copy(stage.at[place.index], landing, out_sem.at[place.z]).start()
+    for row_block in range(RING):
+        await_bytes(out_ref.at[row_block], out_sem.at[row_block])
+    await_bytes(mine, relay_sent_sem)
+    await_bytes(coming, sent_sem)
+    await_bytes(stage.at[pl.ds(0, len(ORDER))], out_sent_sem)
+
+
+def dispatch(picked, gradient, size):
+    _, shard_rows, columns = gradient.shape
+    rows = shard_rows // RING
+    return pl.pallas_call(
+        dispatch_kernel,
+        out_shape=jax.ShapeDtypeStruct((RING, size, size), jnp.float32),
+        in_specs=[
+            pl.BlockSpec(memory_space=pltpu.SMEM),
+            pl.BlockSpec(memory_space=pl.ANY),
+        ],
+        out_specs=pl.BlockSpec(memory_space=pl.ANY),
+        scratch_shapes=[
+            pltpu.VMEM((2, rows, columns // 2), jnp.float32),
+            pltpu.VMEM((rows, columns), jnp.float32),
+            pltpu.VMEM((2, rows, columns // 2), jnp.float32),
+            pltpu.VMEM((2, rows, columns), jnp.float32),
+            pltpu.VMEM((columns // size, rows, size), jnp.float32),
+            pltpu.VMEM((len(ORDER) + 1, rows, size), jnp.float32),
+            pltpu.SemaphoreType.DMA((3,)),
+            pltpu.SemaphoreType.DMA,
+            pltpu.SemaphoreType.DMA,
+            pltpu.SemaphoreType.DMA((2, PARTS)),
+            pltpu.SemaphoreType.DMA((2, 2, PARTS)),
+            pltpu.SemaphoreType.DMA,
+            pltpu.SemaphoreType.DMA((RING,)),
+        ],
+        compiler_params=pltpu.CompilerParams(
+            collective_id=0, has_side_effects=True, vmem_limit_bytes=32 * 2**20
+        ),
+        name="dispatch",
+    )(picked, gradient)
+
+
+def return_kernel(
+    owners_ref, updated_ref, out_ref,
+    came, final, came_sent_sem, came_sem, final_sent_sem, out_sem,
+):
+    place = Place()
+    rows, size = came.shape[1:]
+    greet_all(place)
+
+    def piece(z, k):
+        return updated_ref.at[z, pl.ds(pl.multiple_of(k * rows, rows), rows)]
+
+    landing = came.at[place.index]
+    own = pltpu.make_async_copy(
+        piece(place.z, place.shard * RING + place.y), landing, came_sem
+    )
+    own.start()
+    for offset in ORDER:
+        z, k, device = place.at(*offset)
+        send(piece(z, k), landing, came_sent_sem, came_sem, device)
+    await_bytes(came, came_sem)
+
+    per_quarter = final.shape[2] // size
+    out_rows = out_ref.at[pl.ds(pl.multiple_of(place.y * rows, rows), rows)]
+    for dy in (2, 1, 3, 0):
+        for column in range(per_quarter):
+            owner = owners_ref[place.ys[dy] * per_quarter + column]
+            final[dy, :, pl.ds(column * size, size)] = came[owner]
+        if dy:
+            send(final.at[dy], out_rows, final_sent_sem, out_sem, place.line(dy))
+        else:
+            pltpu.make_async_copy(final.at[dy], out_rows, out_sem).start()
+    await_bytes(out_ref, out_sem)
+    await_bytes(came.at[pl.ds(0, len(ORDER))], came_sent_sem)
+    await_bytes(final.at[pl.ds(0, RING - 1)], final_sent_sem)
+
+
+def give_back(owners, updated, shard_rows, columns):
+    size = updated.shape[2]
+    rows = shard_rows // RING
+    return pl.pallas_call(
+        return_kernel,
+        out_shape=jax.ShapeDtypeStruct((shard_rows, columns), jnp.float32),
+        in_specs=[
+            pl.BlockSpec(memory_space=pltpu.SMEM),
+            pl.BlockSpec(memory_space=pl.ANY),
+        ],
+        out_specs=pl.BlockSpec(memory_space=pl.ANY),
+        scratch_shapes=[
+            pltpu.VMEM((len(ORDER) + 1, rows, size), jnp.float32),
+            pltpu.VMEM((RING, rows, columns), jnp.float32),
+            pltpu.SemaphoreType.DMA,
+            pltpu.SemaphoreType.DMA,
+            pltpu.SemaphoreType.DMA,
+            pltpu.SemaphoreType.DMA,
+        ],
+        compiler_params=pltpu.CompilerParams(
+            collective_id=1, has_side_effects=True, vmem_limit_bytes=32 * 2**20
+        ),
+        name="give_back",
+    )(owners, updated)
 
 
 def split(value):
@@ -98,9 +345,8 @@
     fsdp_index = lax.axis_index("fsdp")
     rep_index = lax.axis_index("rep")
     size = statistics.shape[3]
-    row_blocks, col_blocks = block_owner_table.shape
-    shard_rows = gradient.shape[1]
-    piece_rows = shard_rows // rep_size
+    col_blocks = block_owner_table.shape[1]
+    shard_rows, columns = gradient.shape[1:]
     table = block_owner_table
 
     row_owners = lax.dynamic_index_in_dim(
@@ -108,22 +354,14 @@
     )
     row_of_slot, live = slot_order(table == fsdp_index * rep_size + rep_index)
     matches = row_owners[None, :] == jnp.arange(workers, dtype=jnp.int32)[:, None]
-    columns = jnp.arange(col_blocks, dtype=jnp.int32)
-    picked = jnp.sum(jnp.where(matches, columns[None, :], 0), axis=1)
-
-    summed = lax.psum_scatter(gradient[0], "rep", scatter_dimension=0, tiled=True)
-    pieces = summed.reshape(piece_rows, col_blocks, size).transpose(1, 0, 2)
-    outgoing = jnp.take(pieces, picked, axis=0)
-    arrived = lax.all_to_all(outgoing, ("fsdp", "rep"), split_axis=0, concat_axis=0, tiled=True)
-    blocks = arrived.reshape(row_blocks, size, size)
+    column_index = jnp.arange(col_blocks, dtype=jnp.int32)
+    picked = jnp.sum(jnp.where(matches, column_index[None, :], 0), axis=1)
+
+    blocks = dispatch(picked, gradient, size)
     new_statistics, updated = precondition(
         row_of_slot, live, blocks, statistics, inverse_fourth_roots
     )
-    returning = updated.reshape(workers, piece_rows, size)
-    came_back = lax.all_to_all(returning, ("fsdp", "rep"), split_axis=0, concat_axis=0, tiled=True)
-    ordered = jnp.take(came_back, row_owners, axis=0)
-    quarter = lax.all_to_all(ordered, "rep", split_axis=0, concat_axis=1, tiled=True)
-    direction = quarter.transpose(1, 0, 2).reshape(shard_rows, -1)
+    direction = give_back(row_owners, updated, shard_rows, columns // rep_size)
     return (direction, new_statistics)
 
 

time: 233 us -> 186 us (0.80)
  Pallas kernels: 12.1 us -> 176 us
  waiting for transfers between devices: 153 us -> 0 us
  blocking collectives: 18.7 us -> 0 us
  starting transfers between devices: 16.1 us -> 0 us
  between operations: 14.2 us -> 0.7 us
  local copies, waits for them, and re-layouts: 11.1 us -> 5.76 us
  other arithmetic: 7.37 us -> 3.31 us
    pallas_call x0 -> x2, Pallas kernels: none -> 162 us  [the longest x1 94.5 us: dispatch(): pl.pallas_call(dispatch_kernel, out_shape=jax.ShapeDtypeStruct((RING, siz...]
    all_to_all x2 -> x0, waiting for transfers between devices: 100 us -> none  [the longest x1 51.5 us: on_device(): lax.all_to_all(returning, ('fsdp', 'rep'), split_axis=0, concat_axis=0, t...]
    reduce_scatter x1 -> x0, waiting for transfers between devices: 51.7 us -> none  [on_device(): lax.psum_scatter(gradient[0], 'rep', scatter_dimension=0, tiled=True)]
    all_to_all x1 -> x0, blocking collectives: 18.7 us -> none  [on_device(): lax.all_to_all(ordered, 'rep', split_axis=0, concat_axis=1, tiled=True)]
    all_to_all x2 -> x0, starting transfers between devices: 16 us -> none  [the longest x1 8.91 us: on_device(): lax.all_to_all(outgoing, ('fsdp', 'rep'), split_axis=0, concat_axis=0, ti...]
    gather x2 -> x0, local copies, waits for them, and re-layouts: 5.63 us -> none  [the longest x1 2.83 us: on_device(): outgoing = jnp.take(pieces, picked, axis=0)]
    select_n x4 -> x0, other arithmetic: 4.71 us -> none  [the longest x2 4.56 us: on_device(): outgoing = jnp.take(pieces, picked, axis=0)]
  transfers between devices with their start and end apart: 3 -> 0, of which waited for: 3 -> 0; matrix products, arithmetic and copies ran while one was open for 1% -> 0% of each run, Pallas kernels for 0% -> 0%
where the time goes in v2:
time: 186 us
  Pallas kernels  176 us (95%)
  local copies, waits for them, and re-layouts  5.76 us (3%)
  other arithmetic  3.31 us (2%)
    pallas_call x1, Pallas kernels, dispatch(): pl.pallas_call(dispatch_kernel, out_shape=jax.ShapeDtypeStruct((RING, siz...  94.5 us
    pallas_call x1, Pallas kernels, give_back(): pl.pallas_call(return_kernel, out_shape=jax.ShapeDtypeStruct((shard_rows,...  67.8 us
    pallas_call x1, Pallas kernels, precondition(): pl.pallas_call(block_kernel, grid_spec=pltpu.PrefetchScalarGridSpec(num_s...  13.5 us
    unnamed x5, local copies, waits for them, and re-layouts  5.08 us

profile of v2, /device:TPU:0, one launch (start us, length us, event | category | flops | bytes accessed | tf_op | source)
XLA Modules:
  0.0 185.6 jit_solution(6607150479020091407)
XLA Ops:
  0.7 0.8 compare_reduce_fusion
  1.5 0.6 convert_reduce_fusion
  2.1 0.7 dynamic-slice_bitcast_fusion.owners_ref
  2.8 0.1 select_reduce_fusion.picked_ref
  2.9 0.6 compare_convert_fusion.live_ref
  3.5 0.2 reduce-window.17
  3.7 0.2 reduce-window.16
  3.9 0.7 fusion
  4.6 0.1 select_reduce_fusion.1.row_ref
  4.7 0.0 copy-start.1
  4.7 2.2 %copy-done.1 = f32[1,64,16384]{2,1,0:T(8,128)S(1)} copy-done((f32[1,64,16384]{2,1,0:T(8,128)S(1)}, f32[1,64,16384]{2,1,0:T(8,128)}, u32[]{:S(2)}) %copy-start.1) | copy-done | bytes 4194328
  6.9 94.5 %dispatch.1.g_ref = f32[4,512,512]{2,1,0:T(8,128)S(1)} custom-call(s32[128]{0:T(128)S(1)} %select_reduce_fusion.picked_ref, f32[1,64,16384]{2,1,0:T(8,128)S(1)} %copy-done.1), custom_call_target="tpu_custom_call" | custom-call | tf_op jit(solution)/shard_map/dispatch/pallas_call | solution.py:169
  101.4 0.0 copy-start
  101.4 1.9 %copy-done = f32[4,512,512]{2,1,0:T(8,128)} copy-done((f32[4,512,512]{2,1,0:T(8,128)}, f32[4,512,512]{2,1,0:T(8,128)S(1)}, u32[]{:S(2)}) %copy-start) | copy-done | bytes 4194328
  103.3 13.5 %precondition.1 = (f32[1,4,2,512,512]{4,3,2,1,0:T(8,128)}, f32[4,512,512]{2,1,0:T(8,128)S(1)}) custom-call(s32[4]{0:T(128)S(1)} %select_reduce_fusion.1.row_ref, s32[4]{0:T(128)S(1)} %compare_convert_fusion.live_ref, f32[4,512,512]{2,1,0:T(8,128)} %copy-done, f32[1,4,2,512,512]{4,3,2,1,0:T(8,128)} %stat_ref.1, bf16[1,4,2,512,512]{4,3,2,1,0:T(8,128)(2,1)} %root_ref.1), custom_call_target="tpu_custom_call" | custom-call | tf_op jit(solution)/shard_map/precondition/pallas_call | solution.py:310
  116.9 67.8 %give_back.1 = f32[64,4096]{1,0:T(8,128)S(1)} custom-call(s32[32]{0:T(128)S(1)} %dynamic-slice_bitcast_fusion.owners_ref, f32[4,512,512]{2,1,0:T(8,128)S(1)} %get-tuple-element.4.updated_ref), custom_call_target="tpu_custom_call" | custom-call | tf_op jit(solution)/shard_map/give_back/pallas_call | solution.py:238
  184.7 1.0 copy.7
  (2 shorter events, 0.0 us)
Async XLA Ops:
  4.7 2.2 %copy-start.1 = (f32[1,64,16384]{2,1,0:T(8,128)S(1)}, f32[1,64,16384]{2,1,0:T(8,128)}, u32[]{:S(2)}) copy-start(f32[1,64,16384]{2,1,0:T(8,128)} %grad_ref.1) | copy-start | bytes 12582916
  101.4 1.9 %copy-start = (f32[4,512,512]{2,1,0:T(8,128)}, f32[4,512,512]{2,1,0:T(8,128)S(1)}, u32[]{:S(2)}) copy-start(f32[4,512,512]{2,1,0:T(8,128)S(1)} %dispatch.1.g_ref) | copy-start | bytes 12582916

commit v3 on v1

v3 whole, which is shorter than its diff:
```python
import itertools

import jax
import jax.numpy as jnp
from jax import lax
from jax.experimental import pallas as pl
from jax.experimental.pallas import tpu as pltpu
from jax.sharding import PartitionSpec as P

BETA = 0.9
EPS = 1e-06
MESH = pl.DeviceIdType.MESH
RING = 4
CORES = 2
SHARDS = RING * CORES
PLANE = SHARDS * RING
PARTS = 4


def balanced(offsets):
    left, order, load = sorted(offsets), [], [0.0] * 6

    def hops(offset):
        dz, dx, _, dy = offset
        steps = []
        for d in (dz, dx, dy):
            steps += [1, 1] if d == 2 else [d == 1, d == 3]
        return steps

    while left:
        def cost(offset):
            after = [a + b for a, b in zip(load, hops(offset))]
            return (max(after) - sum(after) / 6, -sum(hops(offset)), offset)

        best = min(left, key=cost)
        left.remove(best)
        order.append(best)
        load = [a + b for a, b in zip(load, hops(best))]
    return order


def offsets(planes):
    every = itertools.product(planes, range(RING), range(CORES), range(RING))
    return [offset for offset in every if any(offset)]


SECOND = balanced(offsets((1, 3)))
ORDER = balanced(offsets((0, 2))) + SECOND


class Place:
    def __init__(self):
        fsdp, self.y = lax.axis_index("fsdp"), lax.axis_index("rep")
        self.z = fsdp // SHARDS
        self.shard = fsdp % SHARDS
        self.chunk = self.shard * RING + self.y
        self.index = fsdp * RING + self.y
        x, c = self.shard // CORES, self.shard % CORES
        self.zs = [lax.rem(self.z + d, RING) for d in range(RING)]
        self.xs = [lax.rem(x + d, RING) * CORES for d in range(RING)]
        self.cs = [c, 1 - c]
        self.ys = [lax.rem(self.y + d, RING) for d in range(RING)]

    def in_plane(self, dx, dc, dy):
        shard = self.xs[dx] + self.cs[dc]
        return shard, self.ys[dy]

    def line(self, dy):
        return {"rep": self.ys[dy]}


def send(src, dst, sent, landed, device):
    pltpu.make_async_remote_copy(
        src_ref=src,
        dst_ref=dst,
        send_sem=sent,
        recv_sem=landed,
        device_id=device,
        device_id_type=MESH,
    ).start()


def await_bytes(like, semaphore):
    pltpu.make_async_copy(like, like, semaphore).wait()


def split(value):
    high = value.astype(jnp.bfloat16)
    low = (value - high.astype(jnp.float32)).astype(jnp.bfloat16)
    return high, low


def dot(a, b):
    return jnp.dot(a, b, preferred_element_type=jnp.float32)


def dot_t(a, b):
    return lax.dot_general(a, b, (((1,), (1,)), ((), ())), preferred_element_type=jnp.float32)


def grafted(matrix, left_root, right_root):
    high, low = split(matrix)
    t_high, t_low = split(dot(left_root, high) + dot(left_root, low))
    shaped = dot(t_high, right_root) + dot(t_low, right_root)
    square_g = jnp.sum(matrix * matrix, keepdims=True) / matrix.size
    square_s = jnp.sum(shaped * shaped, keepdims=True) / matrix.size
    return shaped * (jnp.sqrt(square_g) / jnp.sqrt(square_s + EPS))


def half_grams(matrix):
    high, low = split(matrix)
    half = high * jnp.bfloat16(0.5)
    left = dot_t(high, half) + dot_t(high, low)
    high_t = high.T
    right = dot(high_t, half) + dot(high_t, low)
    return left, right


def pick(index, values):
    result = values[0]
    for k in range(1, len(values)):
        result = jnp.where(index == k, values[k], result)
    return result


def step_kernel(
    table_ref, grad_ref, stat_ref, root_ref, direction_ref, new_ref,
    near, mine, relay, coming, pieces, stage, blocks, roots, returning, came, final,
    picked_row, picked,
    load_sem, sent_sem, relay_sent_sem, relay_sem, coming_sem, out_sent_sem, out_sem,
    back_sent_sem, back_sem, final_sent_sem, final_sem,
):
    place = Place()
    rows, half = mine.shape[0], mine.shape[1] // 2
    width = half // PARTS
    size = stage.shape[2]
    row_blocks, col_blocks = table_ref.shape

    def quarter(dy):
        return pl.ds(pl.multiple_of(place.ys[dy] * rows, rows), rows)

    def grad(dy, side, part=None):
        start, count = (side * half, half) if part is None else (side * half + part * width, width)
        return grad_ref.at[0, quarter(dy), pl.ds(start, count)]

    loads = [
        pltpu.make_async_copy(grad(1, 0), near.at[0], load_sem.at[0]),
        pltpu.make_async_copy(grad(3, 1), near.at[1], load_sem.at[1]),
        pltpu.make_async_copy(grad_ref.at[0, quarter(0)], mine, load_sem.at[2]),
    ]
    root_load = pltpu.make_async_copy(root_ref.at[0], roots, load_sem.at[3])
    stat_load = pltpu.make_async_copy(stat_ref, new_ref, load_sem.at[4])
    for load in loads:
        load.start()

    barrier = pltpu.get_barrier_semaphore()
    for dz, dx, dc, dy in ORDER:
        shard, y = place.in_plane(dx, dc, dy)
        device = (place.zs[dz] * SHARDS + shard, y)
        pl.semaphore_signal(barrier, inc=1, device_id=device, device_id_type=MESH)
    pl.semaphore_wait(barrier, len(ORDER))

    ways = ((1, 0), (3, 1))
    for part in range(PARTS):
        for to, side in ways:
            send(
                grad(2, side, part), relay.at[side, :, pl.ds(part * width, width)],
                sent_sem, relay_sem.at[side, part], place.line(to),
            )
    for part in range(PARTS):
        for to, side in ways:
            columns = pl.ds((1 - side) * half + part * width, width)
            send(
                grad(to, 1 - side, part), coming.at[side, :, columns],
                sent_sem, coming_sem.at[side, 1 - side, part], place.line(to),
            )

    lanes = lax.broadcasted_iota(jnp.int32, picked_row.shape, 1)
    columns_of = jnp.zeros(picked_row.shape, jnp.int32)
    for column in range(col_blocks):
        columns_of = jnp.where(lanes == table_ref[place.z, column], column, columns_of)
    picked_row[...] = columns_of
    picked_copy = pltpu.make_async_copy(picked_row, picked, load_sem.at[5])
    picked_copy.start()

    owned, slot_of_row = [], []
    total = jnp.int32(0)
    for row in range(row_blocks):
        count = jnp.int32(0)
        for column in range(col_blocks):
            count = jnp.where(table_ref[row, column] == place.index, 1, count)
        owned.append(count)
        slot_of_row.append(total)
        total += count
    row_of_slot = []
    for slot in range(row_blocks):
        row_of = jnp.int32(0)
        for row in range(row_blocks):
            row_of += jnp.where(slot_of_row[row] == slot, owned[row] * row, 0)
        row_of_slot.append(row_of)

    for load in loads:
        load.wait()
    for part in range(PARTS):
        for to, side in ways:
            here = pl.ds(part * width, width)
            block = relay.at[side, :, here]
            await_bytes(block, relay_sem.at[side, part])
            relay[side, :, here] += near[side, :, here]
            columns = pl.ds(side * half + part * width, width)
            send(
                block, coming.at[side, :, columns],
                relay_sent_sem, coming_sem.at[side, side, part], place.line(to),
            )
    root_load.start()
    stat_load.start()
    picked_copy.wait()
    for side in range(2):
        for part in range(PARTS):
            columns = pl.ds((1 - side) * half + part * width, width)
            await_bytes(coming.at[side, :, columns], coming_sem.at[side, 1 - side, part])
            mine[:, columns] += coming[side, :, columns]
    for part in range(PARTS):
        for side in range(2):
            start = side * half + part * width
            columns = pl.ds(start, width)
            await_bytes(coming.at[side, :, columns], coming_sem.at[side, side, part])
            for column in range(start, start + width, size):
                at = pl.ds(column, size)
                pieces[column // size] = mine[:, at] + coming[side, :, at]

    chunk = pl.ds(pl.multiple_of(place.chunk * rows, rows), rows)
    landing = blocks.at[place.z, chunk]
    for dz, dx, dc, dy in ORDER:
        shard, y = place.in_plane(dx, dc, dy)
        fsdp = place.zs[dz] * SHARDS + shard
        target = fsdp * RING + y
        stage[target] = pieces[picked[0, target]]
        send(stage.at[target], landing, out_sent_sem, out_sem.at[place.z], (fsdp, y))
    stage[place.index] = pieces[picked[0, place.index]]
    pltpu.make_async_copy(stage.at[place.index], landing, out_sem.at[place.z]).start()

    root_load.wait()
    landing_back = came.at[place.index]

    def two_rows(step, carry):
        planes = [jnp.where(step == 0, 2, 1), jnp.where(step == 0, 0, 3)]
        block_rows = [lax.rem(place.z + dz, RING) for dz in planes]
        for row in block_rows:
            await_bytes(blocks.at[row], out_sem.at[row])
            slot = pick(row, slot_of_row)
            returning[row] = grafted(blocks[row], roots[slot, 0], roots[slot, 1])
        for dz, dx, dc, dy in SECOND:
            row = block_rows[dz // 2]
            shard, y = place.in_plane(dx, dc, dy)
            start = pl.multiple_of((shard * RING + y) * rows, rows)
            piece = returning.at[row, pl.ds(start, rows)]

            def away(piece=piece, row=row, shard=shard, y=y):
                send(piece, landing_back, back_sent_sem, back_sem, (row * SHARDS + shard, y))

            if dz == 1 or any((dx, dc, dy)):
                away()
            else:
                pl.when(step != 0)(away)

                @pl.when(step == 0)
                def _():
                    pltpu.make_async_copy(piece, landing_back, back_sem).start()
        return carry

    lax.fori_loop(0, row_blocks // 2, two_rows, 0)

    stat_load.wait()

    def one_slot(slot, carry):
        left, right = half_grams(blocks[pick(slot, row_of_slot)])
        live = slot < total
        for k, gram in enumerate((left, right)):
            renewed = BETA * new_ref[0, slot, k] + (1.0 - BETA) * (gram + gram.T)
            new_ref[0, slot, k] = jnp.where(live, renewed, 0.0)
        return carry

    lax.fori_loop(0, row_blocks, one_slot, 0)

    await_bytes(came, back_sem)
    per_quarter = final.shape[2] // size
    out_rows = direction_ref.at[pl.ds(pl.multiple_of(place.y * rows, rows), rows)]
    for dy in (2, 1, 3, 0):
        for column in range(per_quarter):
            owner = table_ref[place.z, place.ys[dy] * per_quarter + column]
            final[dy, :, pl.ds(column * size, size)] = came[owner]
        if dy:
            send(final.at[dy], out_rows, final_sent_sem, final_sem, place.line(dy))
        else:
            pltpu.make_async_copy(final.at[dy], out_rows, final_sem).start()

    await_bytes(mine, relay_sent_sem)
    await_bytes(coming, sent_sem)
    await_bytes(stage.at[pl.ds(0, len(ORDER))], out_sent_sem)
    await_bytes(came.at[pl.ds(0, len(ORDER))], back_sent_sem)
    await_bytes(final.at[pl.ds(0, RING - 1)], final_sent_sem)
    await_bytes(direction_ref, final_sem)


def on_device(gradient, block_owner_table, statistics, inverse_fourth_roots):
    size = statistics.shape[3]
    row_blocks, col_blocks = block_owner_table.shape
    _, shard_rows, columns = gradient.shape
    rows = shard_rows // RING
    workers = RING * PLANE
    dma = pltpu.SemaphoreType.DMA
    anywhere = pl.BlockSpec(memory_space=pl.ANY)
    return pl.pallas_call(
        step_kernel,
        out_shape=(
            pltpu.VMEM((shard_rows, columns // RING), jnp.float32),
            pltpu.VMEM(statistics.shape, jnp.float32),
        ),
        in_specs=[pl.BlockSpec(memory_space=pltpu.SMEM), anywhere, anywhere, anywhere],
        out_specs=(pl.BlockSpec(memory_space=pltpu.VMEM),) * 2,
        scratch_shapes=[
            pltpu.VMEM((2, rows, columns // 2), jnp.float32),
            pltpu.VMEM((rows, columns), jnp.float32),
            pltpu.VMEM((2, rows, columns // 2), jnp.float32),
            pltpu.VMEM((2, rows, columns), jnp.float32),
            pltpu.VMEM((col_blocks, rows, size), jnp.float32),
            pltpu.VMEM((workers, rows, size), jnp.float32),
            pltpu.VMEM((row_blocks, size, size), jnp.float32),
            pltpu.VMEM(inverse_fourth_roots.shape[1:], jnp.bfloat16),
            pltpu.VMEM((row_blocks, size, size), jnp.float32),
            pltpu.VMEM((workers, rows, size), jnp.float32),
            pltpu.VMEM((RING, rows, columns // RING), jnp.float32),
            pltpu.VMEM((1, workers), jnp.int32),
            pltpu.SMEM((1, workers), jnp.int32),
            dma((6,)),
            dma,
            dma,
            dma((2, PARTS)),
            dma((2, 2, PARTS)),
            dma,
            dma((row_blocks,)),
            dma,
            dma,
            dma,
            dma,
        ],
        compiler_params=pltpu.CompilerParams(
            collective_id=0, has_side_effects=True, vmem_limit_bytes=44 * 2**20
        ),
        name="shampoo_step",
    )(block_owner_table, gradient, statistics, inverse_fourth_roots)


def solution(mesh):
    in_specs = (
        P("rep", "fsdp", None),
        P(),
        P(("fsdp", "rep"), None, None, None, None),
        P(("fsdp", "rep"), None, None, None, None),
    )
    out_specs = (P("fsdp", "rep"), P(("fsdp", "rep"), None, None, None, None))
    return jax.shard_map(
        on_device, mesh=mesh, in_specs=in_specs, out_specs=out_specs, check_vma=False
    )
```

time: 233 us -> 161 us (0.69)
  waiting for transfers between devices: 153 us -> 0 us
  Pallas kernels: 12.1 us -> 155 us
  blocking collectives: 18.7 us -> 0 us
  starting transfers between devices: 16.1 us -> 0 us
  between operations: 14.2 us -> 0.65 us
  other arithmetic: 7.37 us -> 0 us
  local copies, waits for them, and re-layouts: 11.1 us -> 5.04 us
    pallas_call x1, Pallas kernels: 12.1 us -> 155 us  [on_device(): pl.pallas_call(step_kernel, out_shape=(pltpu.VMEM((shard_rows, columns //...]
    all_to_all x2 -> x0, waiting for transfers between devices: 100 us -> none  [the longest x1 51.5 us: on_device(): lax.all_to_all(returning, ('fsdp', 'rep'), split_axis=0, concat_axis=0, t...]
    reduce_scatter x1 -> x0, waiting for transfers between devices: 51.7 us -> none  [on_device(): lax.psum_scatter(gradient[0], 'rep', scatter_dimension=0, tiled=True)]
    all_to_all x1 -> x0, blocking collectives: 18.7 us -> none  [on_device(): lax.all_to_all(ordered, 'rep', split_axis=0, concat_axis=1, tiled=True)]
    all_to_all x2 -> x0, starting transfers between devices: 16 us -> none  [the longest x1 8.91 us: on_device(): lax.all_to_all(outgoing, ('fsdp', 'rep'), split_axis=0, concat_axis=0, ti...]
    gather x2 -> x0, local copies, waits for them, and re-layouts: 5.63 us -> none  [the longest x1 2.83 us: on_device(): outgoing = jnp.take(pieces, picked, axis=0)]
    select_n x5 -> x0, other arithmetic: 5.36 us -> none  [the longest x2 4.56 us: on_device(): outgoing = jnp.take(pieces, picked, axis=0)]
    unnamed x5 -> x4, local copies, waits for them, and re-layouts: 3.55 us -> 5.04 us
  transfers between devices with their start and end apart: 3 -> 0, of which waited for: 3 -> 0; matrix products, arithmetic and copies ran while one was open for 1% -> 0% of each run, Pallas kernels for 0% -> 0%
where the time goes in v3:
time: 161 us; the launch traced here: 160 us
  Pallas kernels  155 us (96%)
  local copies, waits for them, and re-layouts  5.04 us (3%)
    pallas_call x1, Pallas kernels, on_device(): pl.pallas_call(step_kernel, out_shape=(pltpu.VMEM((shard_rows, columns //...  155 us
    unnamed x4, local copies, waits for them, and re-layouts  5.04 us

profile of v3, /device:TPU:0, one launch (start us, length us, event | category | flops | bytes accessed | tf_op | source)
XLA Modules:
  0.0 160.2 jit_solution(2078086994135841499)
XLA Ops:
  0.6 0.0 copy-start
  0.6 0.7 copy-done
  1.3 154.5 %shampoo_step.1 = (f32[64,4096]{1,0:T(8,128)S(1)}, f32[1,4,2,512,512]{4,3,2,1,0:T(8,128)S(1)}) custom-call(s32[4,32]{1,0:T(4,128)S(1)} %copy-done, f32[1,64,16384]{2,1,0:T(8,128)} %grad_ref.1, f32[1,4,2,512,512]{4,3,2,1,0:T(8,128)} %stat_ref.1, bf16[1,4,2,512,512]{4,3,2,1,0:T(8,128)(2,1)} %root_ref.1), custom_call_target="tpu_custom_call" | custom-call | tf_op jit(solution)/shard_map/shampoo_step/pallas_call | solution.py:314
  155.8 1.0 copy.8
  156.8 3.4 %copy.9 = f32[1,4,2,512,512]{4,3,2,1,0:T(8,128)} copy(f32[1,4,2,512,512]{4,3,2,1,0:T(8,128)S(1)} %get-tuple-element.3) | data formatting | bytes 16777216
Async XLA Ops:
  0.6 0.7 copy-start

commit v4 on v3

--- a/solution.py
+++ b/solution.py
@@ -1,3 +1,4 @@
+import functools
 import itertools
 
 import jax
@@ -14,7 +15,10 @@
 CORES = 2
 SHARDS = RING * CORES
 PLANE = SHARDS * RING
-PARTS = 4
+PARTS = 8
+BACK = (8, 8, 8, 8, 8, 8, 8, 8)
+EARLY = 3
+AHEAD = 3
 
 
 def balanced(offsets):
@@ -44,13 +48,16 @@
     return [offset for offset in every if any(offset)]
 
 
-SECOND = balanced(offsets((1, 3)))
-ORDER = balanced(offsets((0, 2))) + SECOND
+ORDER = balanced(offsets((0, 2))) + balanced(offsets((1, 3)))
+SAME_Y = balanced([offset for offset in offsets(range(RING)) if offset[3] == 0]) + [(0, 0, 0, 0)]
+SAME_Y_ODD = [offset for offset in balanced(offsets((1, 3))) if offset[3] == 0]
+STARTS = [sum(BACK[:k]) for k in range(len(BACK))]
 
 
 class Place:
     def __init__(self):
         fsdp, self.y = lax.axis_index("fsdp"), lax.axis_index("rep")
+        self.fsdp = fsdp
         self.z = fsdp // SHARDS
         self.shard = fsdp % SHARDS
         self.chunk = self.shard * RING + self.y
@@ -125,10 +132,10 @@
 
 def step_kernel(
     table_ref, grad_ref, stat_ref, root_ref, direction_ref, new_ref,
-    near, mine, relay, coming, pieces, stage, blocks, roots, returning, came, final,
+    near, mine, relay, coming, pieces, stage, blocks, roots, returning, far_out, near_out, far_in, merged,
     picked_row, picked,
     load_sem, sent_sem, relay_sent_sem, relay_sem, coming_sem, out_sent_sem, out_sem,
-    back_sent_sem, back_sem, final_sent_sem, final_sem,
+    back_sent_sem, back_sem, far_sent_sem, far_sem, merged_sent_sem, merged_sem, *came,
 ):
     place = Place()
     rows, half = mine.shape[0], mine.shape[1] // 2
@@ -241,7 +248,16 @@
     pltpu.make_async_copy(stage.at[place.index], landing, out_sem.at[place.z]).start()
 
     root_load.wait()
-    landing_back = came.at[place.index]
+    shard_rows = rows * RING
+
+    def rows_back(row, shard, part, remote=True):
+        start = pl.multiple_of(shard * shard_rows + STARTS[part], 8)
+        piece = returning.at[row, pl.ds(start, BACK[part])]
+        landing = came[part].at[place.fsdp]
+        if remote:
+            send(piece, landing, back_sent_sem, back_sem.at[part], (row * SHARDS + shard, place.y))
+        else:
+            pltpu.make_async_copy(piece, landing, back_sem.at[part]).start()
 
     def two_rows(step, carry):
         planes = [jnp.where(step == 0, 2, 1), jnp.where(step == 0, 0, 3)]
@@ -250,57 +266,128 @@
             await_bytes(blocks.at[row], out_sem.at[row])
             slot = pick(row, slot_of_row)
             returning[row] = grafted(blocks[row], roots[slot, 0], roots[slot, 1])
-        for dz, dx, dc, dy in SECOND:
-            row = block_rows[dz // 2]
-            shard, y = place.in_plane(dx, dc, dy)
-            start = pl.multiple_of((shard * RING + y) * rows, rows)
-            piece = returning.at[row, pl.ds(start, rows)]
-
-            def away(piece=piece, row=row, shard=shard, y=y):
-                send(piece, landing_back, back_sent_sem, back_sem, (row * SHARDS + shard, y))
-
-            if dz == 1 or any((dx, dc, dy)):
-                away()
-            else:
-                pl.when(step != 0)(away)
-
-                @pl.when(step == 0)
-                def _():
-                    pltpu.make_async_copy(piece, landing_back, back_sem).start()
+        for part in range(EARLY):
+            for dz, dx, dc, _ in SAME_Y_ODD:
+                row = block_rows[dz // 2]
+                shard = place.in_plane(dx, dc, 0)[0]
+                if dz == 1 or dx or dc:
+                    rows_back(row, shard, part)
+                else:
+                    pl.when(step != 0)(functools.partial(rows_back, row, shard, part))
+                    pl.when(step == 0)(functools.partial(rows_back, row, shard, part, False))
         return carry
 
     lax.fori_loop(0, row_blocks // 2, two_rows, 0)
 
-    stat_load.wait()
-
-    def one_slot(slot, carry):
-        left, right = half_grams(blocks[pick(slot, row_of_slot)])
+    def all_rows_back(part):
+        for dz, dx, dc, _ in SAME_Y:
+            shard = place.in_plane(dx, dc, 0)[0]
+            rows_back(place.zs[dz], shard, part, any((dz, dx, dc)))
+
+    for part in range(EARLY, AHEAD):
+        all_rows_back(part)
+
+    per_quarter = direction_ref.shape[1] // size
+    per_half = per_quarter // 2
+
+    def columns_of_half(side):
+        return [side * per_half + k for k in range(per_half)]
+
+    def owner_of(dy, column):
+        owner = table_ref[place.z, place.ys[dy] * per_quarter + column]
+        return owner // RING, lax.rem(owner % RING - place.y + RING, RING)
+
+    def here(part):
+        return pl.ds(STARTS[part], BACK[part])
+
+    def at(column):
+        return pl.ds(column * size, size)
+
+    half_width = per_half * size
+
+    def send_own(part):
+        await_bytes(came[part], back_sem.at[part])
+        for side, to in ((0, 1), (1, 3)):
+            for k, column in enumerate(columns_of_half(side)):
+                far_out[side, here(part), at(k)] = came[part][owner_of(2, column)[0]]
+            send(
+                far_out.at[side, here(part)], far_in.at[side, here(part)],
+                far_sent_sem, far_sem.at[side, part], place.line(to),
+            )
+        for side, to in ((0, 1), (1, 3)):
+            other = pl.ds((1 - side) * half_width, half_width)
+            for k, column in enumerate(columns_of_half(1 - side)):
+                near_out[side, here(part), at(k)] = came[part][owner_of(to, column)[0]]
+            send(
+                near_out.at[side, here(part)], merged.at[side, here(part), other],
+                far_sent_sem, merged_sem.at[side, 0, part], place.line(to),
+            )
+
+    def send_merged(part):
+        for side, to in ((0, 1), (1, 3)):
+            await_bytes(far_in.at[side, here(part)], far_sem.at[side, part])
+            for k, column in enumerate(columns_of_half(side)):
+                owner, relative = owner_of(to, column)
+                own = came[part][owner]
+                passed = far_in[side, here(part), at(k)]
+                far_in[side, here(part), at(k)] = jnp.where(relative == (to + 2) % RING, passed, own)
+            same = pl.ds(side * half_width, half_width)
+            send(
+                far_in.at[side, here(part)], merged.at[side, here(part), same],
+                merged_sent_sem, merged_sem.at[side, 1, part], place.line(to),
+            )
+
+    def finish(part):
+        for side in range(2):
+            for kind in range(2):
+                columns = pl.ds((side if kind else 1 - side) * half_width, half_width)
+                await_bytes(merged.at[side, here(part), columns], merged_sem.at[side, kind, part])
+        for column in range(per_quarter):
+            owner, relative = owner_of(0, column)
+            by_far = 0 if column < per_half else 1
+            before = merged[0, here(part), at(column)]
+            after = merged[1, here(part), at(column)]
+            from_before = (relative == 3) | ((relative == 2) & (by_far == 0))
+            passed = jnp.where(from_before, before, after)
+            direction_ref[here(part), at(column)] = jnp.where(relative == 0, came[part][owner], passed)
+
+    def renew(slot):
+        left, right = half_grams(blocks[row_of_slot[slot]])
         live = slot < total
         for k, gram in enumerate((left, right)):
             renewed = BETA * new_ref[0, slot, k] + (1.0 - BETA) * (gram + gram.T)
             new_ref[0, slot, k] = jnp.where(live, renewed, 0.0)
-        return carry
-
-    lax.fori_loop(0, row_blocks, one_slot, 0)
-
-    await_bytes(came, back_sem)
-    per_quarter = final.shape[2] // size
-    out_rows = direction_ref.at[pl.ds(pl.multiple_of(place.y * rows, rows), rows)]
-    for dy in (2, 1, 3, 0):
-        for column in range(per_quarter):
-            owner = table_ref[place.z, place.ys[dy] * per_quarter + column]
-            final[dy, :, pl.ds(column * size, size)] = came[owner]
-        if dy:
-            send(final.at[dy], out_rows, final_sent_sem, final_sem, place.line(dy))
-        else:
-            pltpu.make_async_copy(final.at[dy], out_rows, final_sem).start()
+
+    stat_load.wait()
+    for part in range(len(BACK)):
+        send_own(part)
+        if part + AHEAD < len(BACK):
+            all_rows_back(part + AHEAD)
+        if part < row_blocks:
+            renew(part)
+        send_merged(part)
+        if part:
+            finish(part - 1)
+    finish(len(BACK) - 1)
 
     await_bytes(mine, relay_sent_sem)
     await_bytes(coming, sent_sem)
     await_bytes(stage.at[pl.ds(0, len(ORDER))], out_sent_sem)
-    await_bytes(came.at[pl.ds(0, len(ORDER))], back_sent_sem)
-    await_bytes(final.at[pl.ds(0, RING - 1)], final_sent_sem)
-    await_bytes(direction_ref, final_sem)
+    await_bytes(stage.at[pl.ds(0, len(ORDER) + 1 - RING)], back_sent_sem)
+    await_bytes(merged, far_sent_sem)
+    await_bytes(far_in, merged_sent_sem)
+
+
+def store_kernel(direction_ref, new_ref, direction_out, new_out, semaphore):
+    copies = [pltpu.make_async_copy(direction_ref, direction_out, semaphore.at[0])]
+    for slot in range(new_ref.shape[1]):
+        copies.append(
+            pltpu.make_async_copy(new_ref.at[0, slot], new_out.at[0, slot], semaphore.at[slot + 1])
+        )
+    for copy in copies:
+        copy.start()
+    for copy in copies:
+        copy.wait()
 
 
 def on_device(gradient, block_owner_table, statistics, inverse_fourth_roots):
@@ -309,12 +396,13 @@
     _, shard_rows, columns = gradient.shape
     rows = shard_rows // RING
     workers = RING * PLANE
+    quarter = columns // RING
     dma = pltpu.SemaphoreType.DMA
     anywhere = pl.BlockSpec(memory_space=pl.ANY)
-    return pl.pallas_call(
+    direction, new_statistics = pl.pallas_call(
         step_kernel,
         out_shape=(
-            pltpu.VMEM((shard_rows, columns // RING), jnp.float32),
+            pltpu.VMEM((shard_rows, quarter), jnp.float32),
             pltpu.VMEM(statistics.shape, jnp.float32),
         ),
         in_specs=[pl.BlockSpec(memory_space=pltpu.SMEM), anywhere, anywhere, anywhere],
@@ -329,8 +417,10 @@
             pltpu.VMEM((row_blocks, size, size), jnp.float32),
             pltpu.VMEM(inverse_fourth_roots.shape[1:], jnp.bfloat16),
             pltpu.VMEM((row_blocks, size, size), jnp.float32),
-            pltpu.VMEM((workers, rows, size), jnp.float32),
-            pltpu.VMEM((RING, rows, columns // RING), jnp.float32),
+            pltpu.VMEM((2, shard_rows, quarter // 2), jnp.float32),
+            pltpu.VMEM((2, shard_rows, quarter // 2), jnp.float32),
+            pltpu.VMEM((2, shard_rows, quarter // 2), jnp.float32),
+            pltpu.VMEM((2, shard_rows, quarter), jnp.float32),
             pltpu.VMEM((1, workers), jnp.int32),
             pltpu.SMEM((1, workers), jnp.int32),
             dma((6,)),
@@ -341,15 +431,31 @@
             dma,
             dma((row_blocks,)),
             dma,
-            dma,
-            dma,
-            dma,
+            dma((len(BACK),)),
+            dma,
+            dma((2, len(BACK))),
+            dma,
+            dma((2, 2, len(BACK))),
+            *(pltpu.VMEM((workers // RING, part, size), jnp.float32) for part in BACK),
         ],
         compiler_params=pltpu.CompilerParams(
-            collective_id=0, has_side_effects=True, vmem_limit_bytes=44 * 2**20
+            collective_id=0, has_side_effects=True, vmem_limit_bytes=48 * 2**20
         ),
         name="shampoo_step",
     )(block_owner_table, gradient, statistics, inverse_fourth_roots)
+    in_vmem = pl.BlockSpec(memory_space=pltpu.VMEM)
+    return pl.pallas_call(
+        store_kernel,
+        out_shape=(
+            jax.ShapeDtypeStruct(direction.shape, jnp.float32),
+            jax.ShapeDtypeStruct(statistics.shape, jnp.float32),
+        ),
+        in_specs=[in_vmem, in_vmem],
+        out_specs=(anywhere, anywhere),
+        scratch_shapes=[dma((row_blocks + 1,))],
+        compiler_params=pltpu.CompilerParams(vmem_limit_bytes=2**20),
+        name="store",
+    )(direction, new_statistics)
 
 
 def solution(mesh):

time: 161 us -> 157 us (0.975)
  local copies, waits for them, and re-layouts: 5.04 us -> 0 us
  Pallas kernels: 155 us -> 157 us
    unnamed x4 -> x0, local copies, waits for them, and re-layouts: 5.04 us -> none
    pallas_call x1 -> x2, Pallas kernels: 155 us -> 157 us  [the longest x1 153 us: on_device(): pl.pallas_call(step_kernel, out_shape=(pltpu.VMEM((shard_rows, quarter),...]
where the time goes in v4:
time: 157 us
  Pallas kernels  157 us (100%)
    pallas_call x1, Pallas kernels, on_device(): pl.pallas_call(step_kernel, out_shape=(pltpu.VMEM((shard_rows, quarter),...  153 us
    pallas_call x1, Pallas kernels, on_device(): pl.pallas_call(store_kernel, out_shape=(jax.ShapeDtypeStruct(direction.sh...  3.72 us

profile of v4, /device:TPU:0, one launch (start us, length us, event | category | flops | bytes accessed | tf_op | source)
XLA Modules:
  0.0 157.3 jit_solution(1919331116843038006)
XLA Ops:
  0.6 152.8 %shampoo_step.1 = (f32[64,4096]{1,0:T(8,128)S(1)}, f32[1,4,2,512,512]{4,3,2,1,0:T(8,128)S(1)}) custom-call(s32[4,32]{1,0:T(4,128)} %table_ref.1, f32[1,64,16384]{2,1,0:T(8,128)} %grad_ref.1, f32[1,4,2,512,512]{4,3,2,1,0:T(8,128)} %stat_ref.1, bf16[1,4,2,512,512]{4,3,2,1,0:T(8,128)(2,1)} %root_ref.1), custom_call_target="tpu_custom_call" | custom-call | tf_op jit(solution)/shard_map/shampoo_step/pallas_call | solution.py:402
  153.4 3.7 %store.1 = (f32[64,4096]{1,0:T(8,128)}, f32[1,4,2,512,512]{4,3,2,1,0:T(8,128)}) custom-call(f32[64,4096]{1,0:T(8,128)S(1)} %get-tuple-element.4.direction_ref, f32[1,4,2,512,512]{4,3,2,1,0:T(8,128)S(1)} %get-tuple-element.5.new_ref), custom_call_target="tpu_custom_call" | custom-call | tf_op jit(solution)/shard_map/store/pallas_call | solution.py:447

commit v5 on v4

--- a/solution.py
+++ b/solution.py
@@ -15,7 +15,8 @@
 CORES = 2
 SHARDS = RING * CORES
 PLANE = SHARDS * RING
-PARTS = 8
+PARTS = 4
+GATHERED = (8, 8, 8, 8)
 BACK = (8, 8, 8, 8, 8, 8, 8, 8)
 EARLY = 3
 AHEAD = 3
@@ -52,6 +53,7 @@
 SAME_Y = balanced([offset for offset in offsets(range(RING)) if offset[3] == 0]) + [(0, 0, 0, 0)]
 SAME_Y_ODD = [offset for offset in balanced(offsets((1, 3))) if offset[3] == 0]
 STARTS = [sum(BACK[:k]) for k in range(len(BACK))]
+WAYS = ((1, 0), (3, 1))
 
 
 class Place:
@@ -132,33 +134,29 @@
 
 def step_kernel(
     table_ref, grad_ref, stat_ref, root_ref, direction_ref, new_ref,
-    near, mine, relay, coming, pieces, stage, blocks, roots, returning, far_out, near_out, far_in, merged,
-    picked_row, picked,
+    own, relay, coming, pieces, stage, top_relay, top_coming, top_stage,
+    blocks, roots, returning, far_out, near_out, far_in, merged, picked_row, picked,
     load_sem, sent_sem, relay_sent_sem, relay_sem, coming_sem, out_sent_sem, out_sem,
-    back_sent_sem, back_sem, far_sent_sem, far_sem, merged_sent_sem, merged_sem, *came,
+    top_sent_sem, top_relay_sent_sem, top_relay_sem, top_coming_sem,
+    gather_sent_sem, gather_sem, pass_sent_sem, pass_sem, top_out_sent_sem,
+    back_sent_sem, back_sem, far_sent_sem, far_sem, merged_sent_sem, merged_sem, *lists,
 ):
+    gathered, came = lists[: len(GATHERED)], lists[len(GATHERED) :]
     place = Place()
-    rows, half = mine.shape[0], mine.shape[1] // 2
+    shard_rows, all_columns = own.shape
+    top_rows = sum(GATHERED)
+    rows = (shard_rows - top_rows) // RING
+    half = all_columns // 2
     width = half // PARTS
-    size = stage.shape[2]
+    quarter = all_columns // RING
+    side_width = quarter // 2
+    size = blocks.shape[2]
     row_blocks, col_blocks = table_ref.shape
 
-    def quarter(dy):
-        return pl.ds(pl.multiple_of(place.ys[dy] * rows, rows), rows)
-
-    def grad(dy, side, part=None):
-        start, count = (side * half, half) if part is None else (side * half + part * width, width)
-        return grad_ref.at[0, quarter(dy), pl.ds(start, count)]
-
-    loads = [
-        pltpu.make_async_copy(grad(1, 0), near.at[0], load_sem.at[0]),
-        pltpu.make_async_copy(grad(3, 1), near.at[1], load_sem.at[1]),
-        pltpu.make_async_copy(grad_ref.at[0, quarter(0)], mine, load_sem.at[2]),
-    ]
-    root_load = pltpu.make_async_copy(root_ref.at[0], roots, load_sem.at[3])
-    stat_load = pltpu.make_async_copy(stat_ref, new_ref, load_sem.at[4])
-    for load in loads:
-        load.start()
+    own_load = pltpu.make_async_copy(grad_ref.at[0], own, load_sem.at[0])
+    root_load = pltpu.make_async_copy(root_ref.at[0], roots, load_sem.at[1])
+    stat_load = pltpu.make_async_copy(stat_ref, new_ref, load_sem.at[2])
+    own_load.start()
 
     barrier = pltpu.get_barrier_semaphore()
     for dz, dx, dc, dy in ORDER:
@@ -167,27 +165,140 @@
         pl.semaphore_signal(barrier, inc=1, device_id=device, device_id_type=MESH)
     pl.semaphore_wait(barrier, len(ORDER))
 
-    ways = ((1, 0), (3, 1))
-    for part in range(PARTS):
-        for to, side in ways:
-            send(
-                grad(2, side, part), relay.at[side, :, pl.ds(part * width, width)],
+    per_quarter = quarter // size
+    per_half = per_quarter // 2
+
+    def at(column):
+        return pl.ds(column * size, size)
+
+    def top_here(part):
+        return pl.ds(sum(GATHERED[:part]), GATHERED[part])
+
+    def top_columns(dy, side=None):
+        start = pl.multiple_of(place.ys[dy] * quarter, quarter)
+        if side is None:
+            return pl.ds(start, quarter)
+        return pl.ds(pl.multiple_of(start + side * side_width, side_width), side_width)
+
+    def top_blocks(dy, side):
+        return pl.ds(place.ys[dy] * per_quarter + side * per_half, per_half)
+
+    def side_of(side):
+        return pl.ds(side * side_width, side_width)
+
+    def top_send(part):
+        here = top_here(part)
+        for to, side in WAYS:
+            send(
+                grad_ref.at[0, here, top_columns(2, side)], top_relay.at[side, here],
+                top_sent_sem, top_relay_sem.at[side, part], place.line(to),
+            )
+        for to, side in WAYS:
+            send(
+                grad_ref.at[0, here, top_columns(to, 1 - side)],
+                top_coming.at[side, here, side_of(1 - side)],
+                top_sent_sem, top_coming_sem.at[side, 0, part], place.line(to),
+            )
+
+    def top_pass(part):
+        here = top_here(part)
+        for to, side in WAYS:
+            block = top_relay.at[side, here]
+            await_bytes(block, top_relay_sem.at[side, part])
+            top_relay[side, here] += own[here, top_columns(to, side)]
+            send(
+                block, top_coming.at[side, here, side_of(side)],
+                top_relay_sent_sem, top_coming_sem.at[side, 1, part], place.line(to),
+            )
+
+    def top_gather(part):
+        here = top_here(part)
+        for side in range(2):
+            for kind in range(2):
+                columns = side_of(side if kind else 1 - side)
+                await_bytes(top_coming.at[side, here, columns], top_coming_sem.at[side, kind, part])
+        for k in range(per_quarter):
+            start = pl.multiple_of(place.ys[0] * quarter + k * size, size)
+            passed = top_coming[0, here, at(k)] + top_coming[1, here, at(k)]
+            gathered[part][place.ys[0] * per_quarter + k] = own[here, pl.ds(start, size)] + passed
+        for first in range(2):
+            for to, side in WAYS:
+                k = side if first == 0 else 1 - side
+                block = gathered[part].at[top_blocks(0, k)]
+                send(block, block, gather_sent_sem, gather_sem.at[side, k, part], place.line(to))
+
+    def top_gather_on(part):
+        for to, side in WAYS:
+            block = gathered[part].at[top_blocks((to + 2) % RING, side)]
+            await_bytes(block, gather_sem.at[side, side, part])
+            send(block, block, pass_sent_sem, pass_sem.at[side, part], place.line(to))
+
+    def top_dispatch(part):
+        for side, dy in ((0, 3), (1, 1)):
+            rest, far = gathered[part].at[top_blocks(dy, 1 - side)], gathered[part].at[top_blocks(2, side)]
+            await_bytes(rest, gather_sem.at[side, 1 - side, part])
+            await_bytes(far, pass_sem.at[side, part])
+        start = pl.multiple_of(place.shard * shard_rows + sum(GATHERED[:part]), 8)
+        landing = blocks.at[place.z, pl.ds(start, GATHERED[part])]
+        for dz, dx, dc, _ in SAME_Y:
+            fsdp = place.zs[dz] * SHARDS + place.in_plane(dx, dc, 0)[0]
+            piece = top_stage.at[fsdp, top_here(part)]
+            top_stage[fsdp, top_here(part)] = gathered[part][picked[0, fsdp * RING + place.y]]
+            if any((dz, dx, dc)):
+                send(piece, landing, top_out_sent_sem.at[part], out_sem.at[place.z], (fsdp, place.y))
+            else:
+                pltpu.make_async_copy(piece, landing, out_sem.at[place.z]).start()
+
+    def low(dy):
+        return pl.ds(pl.multiple_of(top_rows + place.ys[dy] * rows, 8), rows)
+
+    def low_far(part):
+        for to, side in WAYS:
+            columns = pl.ds(side * half + part * width, width)
+            send(
+                grad_ref.at[0, low(2), columns], relay.at[side, :, pl.ds(part * width, width)],
                 sent_sem, relay_sem.at[side, part], place.line(to),
             )
-    for part in range(PARTS):
-        for to, side in ways:
+
+    def low_near(part):
+        for to, side in WAYS:
             columns = pl.ds((1 - side) * half + part * width, width)
             send(
-                grad(to, 1 - side, part), coming.at[side, :, columns],
-                sent_sem, coming_sem.at[side, 1 - side, part], place.line(to),
-            )
+                grad_ref.at[0, low(to), columns], coming.at[side, :, columns],
+                sent_sem, coming_sem.at[side, 0, part], place.line(to),
+            )
+
+    def low_pass(part):
+        here = pl.ds(part * width, width)
+        for to, side in WAYS:
+            block = relay.at[side, :, here]
+            await_bytes(block, relay_sem.at[side, part])
+            columns = pl.ds(side * half + part * width, width)
+            relay[side, :, here] += own[low(to), columns]
+            send(
+                block, coming.at[side, :, columns],
+                relay_sent_sem, coming_sem.at[side, 1, part], place.line(to),
+            )
+
+    def low_finish(part):
+        for side in range(2):
+            start = side * half + part * width
+            columns = pl.ds(start, width)
+            await_bytes(coming.at[1 - side, :, columns], coming_sem.at[1 - side, 0, part])
+            await_bytes(coming.at[side, :, columns], coming_sem.at[side, 1, part])
+            for column in range(start, start + width, size):
+                here = pl.ds(column, size)
+                pieces[column // size] = own[low(0), here] + coming[0, :, here] + coming[1, :, here]
+
+    top_send(0)
+    top_send(1)
 
     lanes = lax.broadcasted_iota(jnp.int32, picked_row.shape, 1)
     columns_of = jnp.zeros(picked_row.shape, jnp.int32)
     for column in range(col_blocks):
         columns_of = jnp.where(lanes == table_ref[place.z, column], column, columns_of)
     picked_row[...] = columns_of
-    picked_copy = pltpu.make_async_copy(picked_row, picked, load_sem.at[5])
+    picked_copy = pltpu.make_async_copy(picked_row, picked, load_sem.at[3])
     picked_copy.start()
 
     owned, slot_of_row = [], []
@@ -206,38 +317,39 @@
             row_of += jnp.where(slot_of_row[row] == slot, owned[row] * row, 0)
         row_of_slot.append(row_of)
 
-    for load in loads:
-        load.wait()
-    for part in range(PARTS):
-        for to, side in ways:
-            here = pl.ds(part * width, width)
-            block = relay.at[side, :, here]
-            await_bytes(block, relay_sem.at[side, part])
-            relay[side, :, here] += near[side, :, here]
-            columns = pl.ds(side * half + part * width, width)
-            send(
-                block, coming.at[side, :, columns],
-                relay_sent_sem, coming_sem.at[side, side, part], place.line(to),
-            )
+    own_load.wait()
     root_load.start()
     stat_load.start()
     picked_copy.wait()
-    for side in range(2):
-        for part in range(PARTS):
-            columns = pl.ds((1 - side) * half + part * width, width)
-            await_bytes(coming.at[side, :, columns], coming_sem.at[side, 1 - side, part])
-            mine[:, columns] += coming[side, :, columns]
+    top_pass(0)
+    top_send(2)
+    top_pass(1)
+    top_gather(0)
+    top_send(3)
+    top_pass(2)
+    top_gather(1)
+    top_gather_on(0)
+    top_pass(3)
+    top_gather(2)
+    top_gather_on(1)
+    top_dispatch(0)
+    top_gather(3)
+    top_gather_on(2)
+    top_dispatch(1)
+    top_gather_on(3)
     for part in range(PARTS):
-        for side in range(2):
-            start = side * half + part * width
-            columns = pl.ds(start, width)
-            await_bytes(coming.at[side, :, columns], coming_sem.at[side, side, part])
-            for column in range(start, start + width, size):
-                at = pl.ds(column, size)
-                pieces[column // size] = mine[:, at] + coming[side, :, at]
-
-    chunk = pl.ds(pl.multiple_of(place.chunk * rows, rows), rows)
-    landing = blocks.at[place.z, chunk]
+        low_far(part)
+    for part in range(PARTS):
+        low_near(part)
+    top_dispatch(2)
+    top_dispatch(3)
+    for part in range(PARTS):
+        low_pass(part)
+    for part in range(PARTS):
+        low_finish(part)
+
+    start = pl.multiple_of(place.shard * shard_rows + top_rows + place.y * rows, 8)
+    landing = blocks.at[place.z, pl.ds(start, rows)]
     for dz, dx, dc, dy in ORDER:
         shard, y = place.in_plane(dx, dc, dy)
         fsdp = place.zs[dz] * SHARDS + shard
@@ -248,14 +360,13 @@
     pltpu.make_async_copy(stage.at[place.index], landing, out_sem.at[place.z]).start()
 
     root_load.wait()
-    shard_rows = rows * RING
 
     def rows_back(row, shard, part, remote=True):
         start = pl.multiple_of(shard * shard_rows + STARTS[part], 8)
         piece = returning.at[row, pl.ds(start, BACK[part])]
         landing = came[part].at[place.fsdp]
         if remote:
-            send(piece, landing, back_sent_sem, back_sem.at[part], (row * SHARDS + shard, place.y))
+            send(piece, landing, back_sent_sem.at[part], back_sem.at[part], (row * SHARDS + shard, place.y))
         else:
             pltpu.make_async_copy(piece, landing, back_sem.at[part]).start()
 
@@ -287,9 +398,6 @@
     for part in range(EARLY, AHEAD):
         all_rows_back(part)
 
-    per_quarter = direction_ref.shape[1] // size
-    per_half = per_quarter // 2
-
     def columns_of_half(side):
         return [side * per_half + k for k in range(per_half)]
 
@@ -299,9 +407,6 @@
 
     def here(part):
         return pl.ds(STARTS[part], BACK[part])
-
-    def at(column):
-        return pl.ds(column * size, size)
 
     half_width = per_half * size
 
@@ -370,10 +475,17 @@
             finish(part - 1)
     finish(len(BACK) - 1)
 
-    await_bytes(mine, relay_sent_sem)
     await_bytes(coming, sent_sem)
+    await_bytes(relay, relay_sent_sem)
+    await_bytes(top_coming, top_sent_sem)
+    await_bytes(top_relay, top_relay_sent_sem)
+    await_bytes(top_coming, gather_sent_sem)
+    await_bytes(top_relay, pass_sent_sem)
     await_bytes(stage.at[pl.ds(0, len(ORDER))], out_sent_sem)
-    await_bytes(stage.at[pl.ds(0, len(ORDER) + 1 - RING)], back_sent_sem)
+    for part in range(len(GATHERED)):
+        await_bytes(top_stage.at[pl.ds(0, len(SAME_Y) - 1), top_here(part)], top_out_sent_sem.at[part])
+    for part in range(len(BACK)):
+        await_bytes(came[part].at[pl.ds(0, len(SAME_Y) - 1)], back_sent_sem.at[part])
     await_bytes(merged, far_sent_sem)
     await_bytes(far_in, merged_sent_sem)
 
@@ -394,7 +506,8 @@
     size = statistics.shape[3]
     row_blocks, col_blocks = block_owner_table.shape
     _, shard_rows, columns = gradient.shape
-    rows = shard_rows // RING
+    top_rows, tops = sum(GATHERED), len(GATHERED)
+    rows = (shard_rows - top_rows) // RING
     workers = RING * PLANE
     quarter = columns // RING
     dma = pltpu.SemaphoreType.DMA
@@ -408,12 +521,14 @@
         in_specs=[pl.BlockSpec(memory_space=pltpu.SMEM), anywhere, anywhere, anywhere],
         out_specs=(pl.BlockSpec(memory_space=pltpu.VMEM),) * 2,
         scratch_shapes=[
-            pltpu.VMEM((2, rows, columns // 2), jnp.float32),
-            pltpu.VMEM((rows, columns), jnp.float32),
+            pltpu.VMEM((shard_rows, columns), jnp.float32),
             pltpu.VMEM((2, rows, columns // 2), jnp.float32),
             pltpu.VMEM((2, rows, columns), jnp.float32),
             pltpu.VMEM((col_blocks, rows, size), jnp.float32),
             pltpu.VMEM((workers, rows, size), jnp.float32),
+            pltpu.VMEM((2, top_rows, quarter // 2), jnp.float32),
+            pltpu.VMEM((2, top_rows, quarter), jnp.float32),
+            pltpu.VMEM((workers // RING, top_rows, size), jnp.float32),
             pltpu.VMEM((row_blocks, size, size), jnp.float32),
             pltpu.VMEM(inverse_fourth_roots.shape[1:], jnp.bfloat16),
             pltpu.VMEM((row_blocks, size, size), jnp.float32),
@@ -423,7 +538,7 @@
             pltpu.VMEM((2, shard_rows, quarter), jnp.float32),
             pltpu.VMEM((1, workers), jnp.int32),
             pltpu.SMEM((1, workers), jnp.int32),
-            dma((6,)),
+            dma((4,)),
             dma,
             dma,
             dma((2, PARTS)),
@@ -431,11 +546,21 @@
             dma,
             dma((row_blocks,)),
             dma,
+            dma,
+            dma((2, tops)),
+            dma((2, 2, tops)),
+            dma,
+            dma((2, 2, tops)),
+            dma,
+            dma((2, tops)),
+            dma((tops,)),
             dma((len(BACK),)),
+            dma((len(BACK),)),
             dma,
             dma((2, len(BACK))),
             dma,
             dma((2, 2, len(BACK))),
+            *(pltpu.VMEM((col_blocks, part, size), jnp.float32) for part in GATHERED),
             *(pltpu.VMEM((workers // RING, part, size), jnp.float32) for part in BACK),
         ],
         compiler_params=pltpu.CompilerParams(

time: 157 us -> 152 us (0.968); the launches traced: 157 us -> 150 us
  Pallas kernels: 157 us -> 150 us
    pallas_call x1, Pallas kernels: 153 us -> 146 us  [on_device(): pl.pallas_call(step_kernel, out_shape=(pltpu.VMEM((shard_rows, quarter),...]
where the time goes in v5:
time: 152 us; the launch traced here: 150 us
  Pallas kernels  150 us (99%)
    pallas_call x1, Pallas kernels, on_device(): pl.pallas_call(step_kernel, out_shape=(pltpu.VMEM((shard_rows, quarter),...  146 us
    pallas_call x1, Pallas kernels, on_device(): pl.pallas_call(store_kernel, out_shape=(jax.ShapeDtypeStruct(direction.sh...  3.72 us

profile of v5, /device:TPU:0, one launch (start us, length us, event | category | flops | bytes accessed | tf_op | source)
XLA Modules:
  0.0 150.2 jit_solution(17987441257855485059)
XLA Ops:
  0.6 145.8 %shampoo_step.1 = (f32[64,4096]{1,0:T(8,128)S(1)}, f32[1,4,2,512,512]{4,3,2,1,0:T(8,128)S(1)}) custom-call(s32[4,32]{1,0:T(4,128)} %table_ref.1, f32[1,64,16384]{2,1,0:T(8,128)} %grad_ref.1, f32[1,4,2,512,512]{4,3,2,1,0:T(8,128)} %stat_ref.1, bf16[1,4,2,512,512]{4,3,2,1,0:T(8,128)(2,1)} %root_ref.1), custom_call_target="tpu_custom_call" | custom-call | tf_op jit(solution)/shard_map/shampoo_step/pallas_call | solution.py:515
  146.4 3.7 %store.1 = (f32[64,4096]{1,0:T(8,128)}, f32[1,4,2,512,512]{4,3,2,1,0:T(8,128)}) custom-call(f32[64,4096]{1,0:T(8,128)S(1)} %get-tuple-element.4.direction_ref, f32[1,4,2,512,512]{4,3,2,1,0:T(8,128)S(1)} %get-tuple-element.5.new_ref), custom_call_target="tpu_custom_call" | custom-call | tf_op jit(solution)/shard_map/store/pallas_call | solution.py:572
